TPU v7x, 256 devices: a whole 4x4x8 slice. The times are simulated.
256 devices in a mesh: inst: 32 (over x, y, core), tp: 8 (over z).
Axes of the slice: x: 4, y: 4, z: 8, core: 2. Of those that a mesh axis runs over, the one named last changes fastest.
Arguments:
- queries: bfloat16 [32, 4, 8192], P('inst', None, 'tp'), may hold values from -240 to 240
- new_keys: bfloat16 [32, 4, 1024], P('inst', None, 'tp'), may hold values from -6 to 6
- new_values: bfloat16 [32, 4, 1024], P('inst', None, 'tp'), may hold values from -6 to 6
- key_blocks: bfloat16 [256, 2048, 1024], P('inst', None, 'tp'), may hold values from -6 to 6
- value_blocks: bfloat16 [256, 2048, 1024], P('inst', None, 'tp'), may hold values from -6 to 6
- slot_rows: int32 [256], P('inst'), may hold values from 0 to 31
- slot_blocks: int32 [256], P('inst'), may hold values from 0 to 64, as said below
- lengths: int32 [32], replicated, may hold values from 1 to 131072, as said below
- out_weight: bfloat16 [8192, 8192], P('tp', 'inst'), may hold values from -0.0625 to 0.0625
Outputs:
- layer_out: bfloat16 [32, 4, 8192], P('tp', None, 'inst')
Inputs may be any that keep to these rules, and one draw needn't show every extreme that they name: Every block b < ceil(lengths[r] / 2048) of sequence r sits in exactly one slot, with slot_rows = r and slot_blocks = b; every other slot has slot_blocks = 64. The blocks of every sequence but the longest sit in the slots of inst device r; the longest sequence's blocks fill the slots left free on any device. `lengths`: one sequence holds exactly 131072 tokens; every other holds at most 12288.
All inputs are finite; a program needn't handle non-finite values.
Results may differ from a plain program's by a relative error of at most 0.0057.
Values may be sent and summed in bfloat16 or wider, within the bound.
No kernel may reach another device: no remote copies, remote signals or barrier semaphores. Data moves between devices by JAX's collectives and lax.ppermute only.
A program may use at most 64 MiB of HBM per device.

v0:
```python
import jax
import jax.numpy as jnp
from jax import lax
from jax.sharding import PartitionSpec as P

HQ = 8
HD = 128


NEG = -1e30


def merged(shard, axis, combine):
    everything = jax.tree.map(lambda part: lax.all_gather(part, axis), shard)
    first = jax.tree.map(lambda part: part[0], everything)

    def step(k, so_far):
        return combine(so_far, jax.tree.map(lambda part: part[k], everything))

    return lax.fori_loop(1, lax.axis_size(axis), step, first)


def joined(first, second):
    max_one, sum_one, acc_one = first
    max_two, sum_two, acc_two = second
    top = jnp.maximum(max_one, max_two)
    factor_one = jnp.exp(max_one - top)
    factor_two = jnp.exp(max_two - top)
    return (
        top,
        sum_one * factor_one + sum_two * factor_two,
        acc_one * factor_one[..., None] + acc_two * factor_two[..., None],
    )


def body(
    queries,
    new_keys,
    new_values,
    key_blocks,
    value_blocks,
    slot_rows,
    slot_blocks,
    lengths,
    out_weight,
):
    scale = HD ** (-0.5)
    rows_here, steps, query_cols = queries.shape
    groups = query_cols // (HQ * HD)
    slots, block_len, _ = key_blocks.shape
    query_rows = lax.all_gather(queries, "inst", axis=0, tiled=True)
    total_rows = query_rows.shape[0]
    query_heads = query_rows.reshape(total_rows, steps, groups, HQ, HD)
    chosen = query_heads[slot_rows]
    keys = key_blocks.reshape(slots, block_len, groups, HD)
    vals = value_blocks.reshape(slots, block_len, groups, HD)
    scores = (
        jnp.einsum("stghd,sbgd->stghb", chosen, keys, preferred_element_type=jnp.float32) * scale
    )
    position = slot_blocks[:, None] * block_len + jnp.arange(block_len, dtype=jnp.int32)[None, :]
    valid = (position < lengths[slot_rows][:, None])[:, None, None, None, :]
    scores = jnp.where(valid, scores, NEG)
    slot_max = jnp.max(scores, axis=-1)
    weights = jnp.where(valid, jnp.exp(scores - slot_max[..., None]), 0.0)
    slot_sum = jnp.sum(weights, axis=-1)
    slot_acc = jnp.einsum(
        "stghb,sbgd->stghd", weights.astype(jnp.bfloat16), vals, preferred_element_type=jnp.float32
    )
    onehot = slot_rows[:, None] == jnp.arange(total_rows, dtype=jnp.int32)[None, :]
    local_max = jnp.max(jnp.where(onehot[:, :, None, None, None], slot_max[:, None], NEG), axis=0)
    slot_factor = jnp.exp(slot_max - local_max[slot_rows])
    onehot_f = onehot.astype(jnp.float32)
    local_sum = jnp.einsum(
        "sr,stgh->rtgh", onehot_f, slot_sum * slot_factor, precision=lax.Precision.HIGHEST
    )
    local_acc = jnp.einsum(
        "sr,stghd->rtghd",
        onehot_f,
        slot_acc * slot_factor[..., None],
        precision=lax.Precision.HIGHEST,
    )
    own_query = queries.reshape(rows_here, steps, groups, HQ, HD)
    fresh_keys = new_keys.reshape(rows_here, steps, groups, HD)
    fresh_vals = new_values.reshape(rows_here, steps, groups, HD)
    own_scores = (
        jnp.einsum("rtghd,rugd->rtghu", own_query, fresh_keys, preferred_element_type=jnp.float32)
        * scale
    )
    causal = (jnp.arange(steps)[:, None] >= jnp.arange(steps)[None, :])[None, :, None, None, :]
    own_scores = jnp.where(causal, own_scores, NEG)
    own_max = jnp.max(own_scores, axis=-1)
    own_weights = jnp.where(causal, jnp.exp(own_scores - own_max[..., None]), 0.0)
    own_sum = jnp.sum(own_weights, axis=-1)
    own_acc = jnp.einsum(
        "rtghu,rugd->rtghd",
        own_weights.astype(jnp.bfloat16),
        fresh_vals,
        preferred_element_type=jnp.float32,
    )
    first_row = lax.axis_index("inst") * rows_here
    row_ids = jnp.arange(total_rows, dtype=jnp.int32)
    is_mine = (row_ids >= first_row) & (row_ids < first_row + rows_here)
    picker = jnp.clip(row_ids - first_row, 0, rows_here - 1)
    mine = is_mine[:, None, None, None]
    spread_max = jnp.where(mine, own_max[picker], NEG)
    spread_sum = jnp.where(mine, own_sum[picker], 0.0)
    spread_acc = jnp.where(mine[..., None], own_acc[picker], 0.0)
    combined = joined((local_max, local_sum, local_acc), (spread_max, spread_sum, spread_acc))
    top, total, weighted = merged(combined, "inst", joined)
    attended_all = (
        (weighted / total[..., None]).astype(jnp.bfloat16).reshape(total_rows, steps, query_cols)
    )
    out_cols = out_weight.shape[1]
    share_rows = total_rows // lax.axis_size("tp")
    product = jnp.dot(
        attended_all.reshape(lax.axis_size("tp") * share_rows * steps, query_cols),
        out_weight,
        preferred_element_type=jnp.float32,
    )
    summed = lax.psum_scatter(
        product.reshape(lax.axis_size("tp") * share_rows, steps, out_cols),
        "tp",
        scatter_dimension=0,
        tiled=True,
    )
    return summed.astype(jnp.bfloat16)


def solution(mesh):
    in_specs = (
        P("inst", None, "tp"),
        P("inst", None, "tp"),
        P("inst", None, "tp"),
        P("inst", None, "tp"),
        P("inst", None, "tp"),
        P("inst"),
        P("inst"),
        P(),
        P("tp", "inst"),
    )
    out_specs = P("tp", None, "inst")
    return jax.shard_map(body, mesh=mesh, in_specs=in_specs, out_specs=out_specs, check_vma=False)
```

profile of v0, /device:TPU:2, one launch (start us, length us, event | category | flops | bytes accessed | tf_op | source)
XLA Modules:
  0.0 228.0 jit_solution(649929564254602735)
XLA Ops:
  6.5 0.7 compare_select_fusion
  7.3 0.7 iota_compare_fusion
  8.0 0.7 broadcast_multiply_fusion
  8.7 24.8 %all_gather.19 = bf16[32,4,1024]{2,1,0:T(4,128)(2,1)S(1)} all-gather(bf16[1,4,1024]{2,1,0:T(4,128)(2,1)} %param.11), channel_id=1, replica_groups=mesh['inst'=32,'tp'=8] {'inst'}, dimensions={0}, use_global_device_ids=true | all-gather | bytes 270336 | tf_op jit(solution)/shard_map/all_gather | solution.py:51
  33.5 1.3 gather_fusion
  35.5 3.7 %fusion.64 = (f32[8,4,8]{2,1,0:T(4,128)S(1)}, f32[8,4,1,8,2048]{4,3,1,0,2:T(8,128)S(1)}) fusion(bf16[8,4,8,128]{3,2,1,0:T(8,128)(2,1)S(1)} %gather_fusion.1, bf16[8,2048,128]{2,1,0:T(8,128)(2,1)} %param.14, pred[8,2048]{1,0:T(8,128)(4,1)S(1)} %add_compare_fusion), kind=kOutput, calls=%fused_computation.81 | convolution fusion | flops 135790336 | bytes 6374400 | tf_op jit(solution)/shard_map/stghd,sbgd->stghb/dot_general | solution.py:58
  40.0 0.6 gather_fusion.2
  41.1 3.1 %fusion.31 = f32[8,4,8,128]{3,2,1,0:T(8,128)S(1)} fusion(bf16[8,2048,128]{2,1,0:T(8,128)(2,1)} %param.15, f32[8,4,1,8,2048]{4,3,1,0,2:T(8,128)S(1)} %get-tuple-element.237, f32[8,4,8]{2,1,0:T(4,128)S(1)} %get-tuple-element.236, pred[8,2048]{1,0:T(8,128)(4,1)S(1)} %add_compare_fusion, f32[8,4,8]{2,1,0:T(4,128)S(1)} %bitcast.168), kind=kOutput, calls=%fused_computation.30 | convolution fusion | flops 135823360 | bytes 6440960 | tf_op jit(solution)/shard_map/stghb,sbgd->stghd/dot_general | solution.py:66
  44.4 1.3 fusion.24
  46.1 25.8 %all-gather = f32[1024,4,8]{2,1,0:T(4,128)S(1)} all-gather(f32[32,4,8]{2,1,0:T(4,128)S(1)} %copy.65), channel_id=2, replica_groups=mesh['inst'=32,'tp'=8] {'inst'}, dimensions={0}, use_global_device_ids=true | all-gather | bytes 135168 | tf_op jit(solution)/shard_map/all_gather | solution.py:14
  72.0 0.8 copy.72
  72.9 0.6 dynamic-slice
  74.1 23.9 %all_gather.20 = f32[32,32,4,1,8]{1,4,3,2,0:T(8,128)S(1)} all-gather(f32[1,32,4,1,8]{1,4,3,2,0:T(8,128)S(1)} %fusion.48), channel_id=1, replica_groups=mesh['inst'=32,'tp'=8] {'inst'}, dimensions={0}, use_global_device_ids=true | all-gather | bytes 135168 | tf_op jit(solution)/shard_map/all_gather | solution.py:14
  98.0 28.9 %all-gather.4.cloned.1.call-done = f32[1024,4,8,128]{3,0,2,1:T(8,128)} async-done(((f32[32,4,8,128]{3,0,2,1:T(8,128)}), f32[1024,4,8,128]{3,0,2,1:T(8,128)}) %all-gather.4.cloned.1.call-update) | async-done | bytes 16777232 | tf_op jit(solution)/shard_map/all_gather | solution.py:14
  126.8 1.1 slice_bitcast_fusion
  128.2 60.1 %while.19 = (s32[]{:T(128)}, f32[32,4,1,8]{0,3,2,1:T(8,128)S(1)}, f32[32,4,1,8]{0,3,2,1:T(8,128)S(1)}, f32[32,4,1,8,128]{4,3,2,1,0:T(8,128)S(1)}, f32[32,32,4,1,...) while((s32[]{:T(128)}, f32[32,4,1,8]{0,3,2,1:T(8,128)S(1)}, ...), condition=%wide.region_6.7_spmd, body=%wide.region_5.6_spmd.sunk | while | flops 400389 | bytes 2699419 | solution.py:20
  128.5 1.1 constant_dynamic-slice_fusion.2
  129.6 0.6 fusion.71
  130.4 1.1 constant_dynamic-slice_fusion.2
  131.5 0.6 fusion.71
  132.4 1.1 constant_dynamic-slice_fusion.2
  133.5 0.6 fusion.71
  134.3 1.1 constant_dynamic-slice_fusion.2
  135.4 0.6 fusion.71
  136.2 1.1 constant_dynamic-slice_fusion.2
  137.3 0.6 fusion.71
  138.2 1.1 constant_dynamic-slice_fusion.2
  139.3 0.6 fusion.71
  140.1 1.1 constant_dynamic-slice_fusion.2
  141.2 0.6 fusion.71
  142.1 1.1 constant_dynamic-slice_fusion.2
  143.1 0.6 fusion.71
  144.0 1.1 constant_dynamic-slice_fusion.2
  145.1 0.6 fusion.71
  145.9 1.1 constant_dynamic-slice_fusion.2
  147.0 0.6 fusion.71
  147.9 1.1 constant_dynamic-slice_fusion.2
  149.8 1.1 constant_dynamic-slice_fusion.2
  150.9 0.6 fusion.71
  151.7 1.1 constant_dynamic-slice_fusion.2
  153.7 1.1 constant_dynamic-slice_fusion.2
  155.6 1.1 constant_dynamic-slice_fusion.2
  156.7 0.6 fusion.71
  157.6 1.1 constant_dynamic-slice_fusion.2
  159.5 1.1 constant_dynamic-slice_fusion.2
  161.4 1.1 constant_dynamic-slice_fusion.2
  163.4 1.1 constant_dynamic-slice_fusion.2
  165.3 1.1 constant_dynamic-slice_fusion.2
  166.4 0.6 fusion.71
  167.3 1.1 constant_dynamic-slice_fusion.2
  169.2 1.1 constant_dynamic-slice_fusion.2
  171.1 1.1 constant_dynamic-slice_fusion.2
  172.2 0.6 fusion.71
  173.1 1.1 constant_dynamic-slice_fusion.2
  175.0 1.1 constant_dynamic-slice_fusion.2
  177.0 1.1 constant_dynamic-slice_fusion.2
  178.9 1.1 constant_dynamic-slice_fusion.2
  180.8 1.1 constant_dynamic-slice_fusion.2
  182.8 1.1 constant_dynamic-slice_fusion.2
  184.7 1.1 constant_dynamic-slice_fusion.2
  186.6 1.1 constant_dynamic-slice_fusion.2
  187.7 0.6 fusion.71
  189.0 31.5 %all-reduce.2 = bf16[32,4,256]{2,0,1:T(8,128)(2,1)S(1)} all-reduce(f32[32,4,256]{2,0,1:T(8,128)S(1)} %fusion.41), channel_id=4, replica_groups=mesh['inst'=32,'tp'=8] {'tp'}, use_global_device_ids=true, to_apply=%region_7.8.clone | all-reduce | flops 32768 | bytes 196608
  220.6 0.6 copy.76
  (213 shorter events, 19.4 us)
Async XLA Ops:
  6.5 182.2 %copy-start = (bf16[1024,256]{1,0:T(8,128)(2,1)S(1)}, bf16[1024,256]{1,0:T(8,128)(2,1)}, u32[]{:S(2)}) copy-start(bf16[1024,256]{1,0:T(8,128)(2,1)} %param.19) | copy-start | bytes 1572868
  6.5 120.3 %all-gather.4.cloned.1.call-start = ((), (), s32[]{:S(2)}) async-start(), calls=%async_computation | async-start | bytes 17301504 | tf_op jit(solution)/shard_map/all_gather | solution.py:14
  39.2 1.4 copy-start.1
  39.2 1.4 copy-start.2
  41.1 3.1 %copy-start.3 = (bf16[1,4,128]{2,1,0:T(4,128)(2,1)S(1)}, bf16[1,4,128]{2,1,0:T(4,128)(2,1)}, u32[]{:S(2)}) copy-start(bf16[1,4,128]{2,1,0:T(4,128)(2,1)} %param.13) | copy-start | bytes 3076
  41.1 3.3 %copy-start.4 = (s32[8]{0:T(128)S(1)}, s32[8]{0:T(128)}, u32[]{:S(2)}) copy-start(s32[8]{0:T(128)} %param.16) | copy-start | bytes 100
  46.1 26.7 %copy-start.5 = (u32[256]{0:T(256)S(1)}, u32[256]{0:T(256)}, u32[]{:S(2)}) copy-start(u32[256]{0:T(256)} %constant.71) | copy-start | bytes 3076
Sparse Core Ops, SparseCore 0:
  45.9 80.9 all-gather.3
where the time goes:
time: 230 us; the launch traced here: 228 us
  blocking collectives  106 us (46%)
  local copies, waits for them, and re-layouts  45.7 us (20%)
  waiting for transfers between devices  28.9 us (13%)
  other arithmetic  22.4 us (10%)
  between operations  14.2 us (6%)
  matrix products  8.87 us (4%)
    all_gather x2, blocking collectives, merged(): everything = jax.tree.map(lambda part: lax.all_gather(part, axis), shard)  49.7 us
    dynamic_slice x31, local copies, waits for them, and re-layouts, step(): return combine(so_far, jax.tree.map(lambda part: part[k], everything))  33.8 us
    unnamed x1, blocking collectives  31.5 us
    all_gather x1, waiting for transfers between devices, merged(): everything = jax.tree.map(lambda part: lax.all_gather(part, axis), shard)  28.9 us
    all_gather x1, blocking collectives, body(): query_rows = lax.all_gather(queries, 'inst', axis=0, tiled=True)  24.8 us
    add x31, other arithmetic, joined(): acc_one * factor_one[..., None] + acc_two * factor_two[..., None]  17.8 us
  transfers between devices with their start and end apart: 1, of which 1 were waited for; matrix products, arithmetic and copies ran while one was open for 1% of the time, Pallas kernels for 0%

commit v1 on v0

v1 whole, which is shorter than its diff:
```python
import functools
import math

import jax
import jax.numpy as jnp
from jax import lax
from jax.experimental import pallas as pl
from jax.experimental.pallas import tpu as pltpu
from jax.sharding import PartitionSpec as P

HQ = 8
HD = 128
WIDTH = HQ * HD
NEG = -1e30
FLOOR = -1e29
C = HD ** (-0.5) / math.log(2.0)
PIECES = 3
CORES = 2


def longest_row(lengths_ref):
    row, most = jnp.int32(0), lengths_ref[0]
    for r in range(1, lengths_ref.shape[0]):
        here = lengths_ref[r]
        row = jnp.where(here > most, r, row)
        most = jnp.maximum(here, most)
    return row


def pieces_of(x):
    parts = []
    for _ in range(PIECES):
        part = x.astype(jnp.bfloat16).astype(jnp.float32)
        parts.append(part)
        x = x - part
    return parts


def rows_of_heads(q):
    return jnp.concatenate([q[:, h * HD : (h + 1) * HD] for h in range(HQ)], axis=0)


def spread_kernel(
    block_len,
    me_ref,
    rows_hbm,
    blocks_hbm,
    lengths_hbm,
    query_hbm,
    new_key_hbm,
    new_value_hbm,
    other_ref,
    spread_ref,
    query_ref,
    new_key_ref,
    new_value_ref,
    plan_ref,
    rows_ref,
    blocks_ref,
    lengths_ref,
    sems,
):
    slots = rows_ref.shape[0]
    copies = [
        pltpu.make_async_copy(source, target, sems.at[k])
        for k, (source, target) in enumerate(
            [
                (lengths_hbm, lengths_ref),
                (query_hbm.at[0], query_ref),
                (rows_hbm, rows_ref),
                (blocks_hbm, blocks_ref),
                (new_key_hbm.at[0], new_key_ref),
                (new_value_hbm.at[0], new_value_ref),
            ]
        )
    ]
    for copy in copies:
        copy.start()
    for copy in copies:
        copy.wait()
    me = me_ref[0]
    longest = longest_row(lengths_ref)
    asked = jnp.where(
        me // CORES * CORES + (CORES - 1 - me % CORES) == longest,
        other_ref[0].astype(jnp.float32),
        query_ref[...].astype(jnp.float32),
    ).astype(jnp.bfloat16)
    spread_ref[...] = jnp.broadcast_to(asked[None], spread_ref.shape)
    plan_ref[0] = longest
    plan_ref[1] = me
    for s in range(slots):
        row = rows_ref[s]
        in_long = row == longest
        valid = jnp.clip(lengths_ref[row] - blocks_ref[s] * block_len, 0, block_len)
        plan_ref[2 + s] = in_long.astype(jnp.int32)
        plan_ref[2 + slots + s] = jnp.where(in_long | (row == me), valid, 0)


def attend_kernel(
    plan_ref,
    asked_ref,
    query_ref,
    new_key_ref,
    new_value_ref,
    key_ref,
    value_ref,
    out_ref,
    queries,
    scores,
):
    slots, block_len, _ = key_ref.shape
    steps = query_ref.shape[0]
    heads = HQ * steps
    longest = plan_ref[0]
    mine = plan_ref[1] == longest
    own_query = rows_of_heads(query_ref[...].astype(jnp.float32))
    queries[0] = own_query.astype(jnp.bfloat16)
    queries[1] = rows_of_heads(asked_ref[longest // CORES].astype(jnp.float32)).astype(jnp.bfloat16)

    column = lax.broadcasted_iota(jnp.int32, (heads, block_len), 1)
    tops = []
    for s in range(slots):
        score = lax.dot_general(
            queries[plan_ref[2 + s]],
            key_ref[s],
            (((1,), (1,)), ((), ())),
            preferred_element_type=jnp.float32,
        )
        score = jnp.where(column < plan_ref[2 + slots + s], score, NEG)
        scores[s] = score
        tops.append(jnp.maximum(jnp.max(score, axis=1, keepdims=True), FLOOR))

    step_of = lax.broadcasted_iota(jnp.int32, (heads, 1), 0) % steps
    fresh = []
    for u in range(steps):
        score = jnp.sum(
            own_query * new_key_ref[u : u + 1, :].astype(jnp.float32), axis=1, keepdims=True
        )
        fresh.append(jnp.where(step_of >= u, score, NEG))
    top = functools.reduce(jnp.maximum, fresh)
    total = jnp.zeros_like(top)
    acc = jnp.zeros((heads, HD), jnp.float32)
    for u in range(steps):
        weight = jnp.exp2((fresh[u] - top) * C)
        total += weight
        acc += weight.astype(jnp.bfloat16).astype(jnp.float32) * new_value_ref[
            u : u + 1, :
        ].astype(jnp.float32)
    parts = [(mine, top, total, acc)]

    for s in range(slots):
        weights = jnp.exp2((scores[s] - tops[s]) * C)
        total = jnp.sum(weights, axis=1, keepdims=True)
        acc = jnp.dot(
            weights.astype(jnp.bfloat16), value_ref[s], preferred_element_type=jnp.float32
        )
        parts.append((plan_ref[2 + s] == 1, tops[s], total, acc))

    merged = []
    for wanted in (False, True):
        best = functools.reduce(
            jnp.maximum, [jnp.where(in_long == wanted, top, FLOOR) for in_long, top, _, _ in parts]
        )
        sum_all = jnp.zeros_like(best)
        acc_all = jnp.zeros((heads, HD), jnp.float32)
        for in_long, top, total, acc in parts:
            factor = jnp.where(in_long == wanted, jnp.exp2(jnp.minimum(top - best, 0.0) * C), 0.0)
            sum_all += factor * total
            acc_all += factor * acc
        merged.append((best, sum_all, acc_all))

    _, own_sum, own_acc = merged[0]
    attended = own_acc / jnp.where(own_sum > 0.0, own_sum, 1.0)
    long_top, long_sum, long_acc = merged[1]
    stats = pieces_of(long_top) + pieces_of(long_sum)
    lane = lax.broadcasted_iota(jnp.int32, (steps, HD), 1)
    packed = jnp.zeros((steps, HD), jnp.float32)
    for h in range(HQ):
        rows = slice(h * steps, (h + 1) * steps)
        for k, piece in enumerate(stats):
            packed = jnp.where(lane == k * HQ + h, piece[rows], packed)
    heads_of = lambda x: [x[h * steps : (h + 1) * steps] for h in range(HQ)]
    sent = jnp.concatenate(heads_of(attended) + heads_of(long_acc) + [packed], axis=1)
    out_ref[...] = sent.astype(jnp.bfloat16)


def project_kernel(steps, plan_ref, mine_ref, other_ref, weight_ref, out_ref):
    half, _ = mine_ref.shape
    rows = CORES * half
    longest = plan_ref[0]
    first = plan_ref[1] % CORES == 0
    both = lambda cols: jnp.concatenate([mine_ref[:, cols], other_ref[:, cols]], axis=0)
    stats = both(slice(2 * WIDTH, 2 * WIDTH + HD))
    lane = lax.broadcasted_iota(jnp.int32, (HD, WIDTH), 0)
    chosen = lane % HQ == lax.broadcasted_iota(jnp.int32, (HD, WIDTH), 1) // HD
    split = PIECES * HQ
    pick_top = jnp.where(chosen & (lane < split), 1.0, 0.0).astype(jnp.bfloat16)
    pick_sum = jnp.where(chosen & (lane >= split), 1.0, 0.0).astype(jnp.bfloat16)
    tops = jnp.dot(stats, pick_top, preferred_element_type=jnp.float32)
    sums = jnp.dot(stats, pick_sum, preferred_element_type=jnp.float32)
    accs = both(slice(WIDTH, 2 * WIDTH)).astype(jnp.float32)

    pair = 2 * steps
    fold = lambda x: x.reshape(-1, pair, x.shape[-1])
    best = jnp.max(fold(tops), axis=0)
    best = jnp.maximum(best, pltpu.roll(best, steps, 0))
    factor = jnp.exp2((fold(tops) - best[None]) * C)
    total = jnp.sum(factor * fold(sums), axis=0)
    weighted = jnp.sum(factor * fold(accs), axis=0)
    total = total + pltpu.roll(total, steps, 0)
    weighted = weighted + pltpu.roll(weighted, steps, 0)
    merged = weighted / total

    own = mine_ref[:, :WIDTH].astype(jnp.float32)
    other = other_ref[:, :WIDTH].astype(jnp.float32)
    own, other = jnp.where(first, own, other), jnp.where(first, other, own)
    shape = (half // pair, pair, WIDTH)
    chip = lax.broadcasted_iota(jnp.int32, shape, 0) * (pair // steps)
    chip = chip + lax.broadcasted_iota(jnp.int32, shape, 1) // steps
    attended = [
        jnp.where(chip * CORES + core == longest, merged[None], fold(part)).reshape(half, WIDTH)
        for core, part in enumerate((own, other))
    ]
    product = jnp.dot(
        jnp.concatenate(attended, axis=0).astype(jnp.bfloat16),
        weight_ref[...],
        preferred_element_type=jnp.float32,
    )
    shares, each, cols = out_ref.shape
    product = product.reshape(CORES, shares, each // CORES, cols)
    out_ref[...] = jnp.concatenate([product[c] for c in range(CORES)], axis=1).astype(out_ref.dtype)


def add_kernel(shares_ref, out_ref):
    rows, steps, _ = out_ref.shape
    summed = jnp.sum(shares_ref[...].astype(jnp.float32), axis=0)
    for core in range(CORES):
        for k in range(rows // CORES):
            at = (core * (rows // CORES) + k) * steps
            out_ref[k * CORES + core] = summed[at : at + steps].astype(out_ref.dtype)


SMEM = pl.BlockSpec(memory_space=pltpu.SMEM)
VMEM = pl.BlockSpec(memory_space=pltpu.VMEM)
HBM = pl.BlockSpec(memory_space=pltpu.HBM)


def near(x):
    return pltpu.with_memory_space_constraint(x, pltpu.VMEM)


def far(x):
    return pltpu.with_memory_space_constraint(x, pltpu.HBM)


def body(
    queries,
    new_keys,
    new_values,
    key_blocks,
    value_blocks,
    slot_rows,
    slot_blocks,
    lengths,
    out_weight,
):
    _, steps, width = queries.shape
    slots, block_len, _ = key_blocks.shape
    heads = HQ * steps
    devices = lax.axis_size("inst")
    chips = devices // CORES
    shares = lax.axis_size("tp")
    me = lax.axis_index("inst").astype(jnp.int32).reshape(1)
    same_core = [[chip * CORES + core for chip in range(chips)] for core in range(CORES)]
    core_pairs = [(i, i ^ 1) for i in range(devices)]
    params = pltpu.CompilerParams(vmem_limit_bytes=24 * 1024 * 1024)

    def over_chips(x):
        return lax.all_to_all(x, "inst", 0, 0, tiled=True, axis_index_groups=same_core)

    spread, query, new_key, new_value, plan = pl.pallas_call(
        functools.partial(spread_kernel, block_len),
        out_shape=[
            pltpu.VMEM((chips, steps, width), jnp.bfloat16),
            pltpu.VMEM((steps, width), jnp.bfloat16),
            pltpu.VMEM((steps, HD), jnp.bfloat16),
            pltpu.VMEM((steps, HD), jnp.bfloat16),
            pltpu.SMEM((2 + 2 * slots,), jnp.int32),
        ],
        in_specs=[SMEM] + [HBM] * 6 + [VMEM],
        out_specs=[VMEM] * 4 + [SMEM],
        scratch_shapes=[
            pltpu.SMEM((slots,), jnp.int32),
            pltpu.SMEM((slots,), jnp.int32),
            pltpu.SMEM(lengths.shape, jnp.int32),
            pltpu.SemaphoreType.DMA((6,)),
        ],
        compiler_params=params,
        cost_estimate=pl.CostEstimate(
            flops=40_000_000_000, bytes_accessed=60_000_000, transcendentals=0
        ),
        name="spread",
    )(
        me,
        *map(far, (slot_rows, slot_blocks, lengths, queries, new_keys, new_values)),
        lax.ppermute(queries, "inst", core_pairs),
    )
    plan = pltpu.with_memory_space_constraint(plan, pltpu.SMEM)
    asked = over_chips(spread)
    sent_cols = 2 * width + HD
    partial = pl.pallas_call(
        attend_kernel,
        out_shape=jax.ShapeDtypeStruct((steps, sent_cols), jnp.bfloat16),
        in_specs=[SMEM] + [VMEM] * 6,
        out_specs=VMEM,
        scratch_shapes=[
            pltpu.VMEM((2, heads, HD), jnp.bfloat16),
            pltpu.VMEM((slots, heads, block_len), jnp.float32),
        ],
        compiler_params=params,
        cost_estimate=pl.CostEstimate(
            flops=300_000_000, bytes_accessed=9_000_000, transcendentals=600_000
        ),
        name="attend",
    )(
        plan,
        asked,
        near(query),
        near(new_key),
        near(new_value),
        near(key_blocks),
        near(value_blocks),
    )
    everyone = over_chips(jnp.broadcast_to(partial[None], (chips, steps, sent_cols)))
    everyone = everyone.reshape(chips * steps, sent_cols)
    share = pl.pallas_call(
        functools.partial(project_kernel, steps),
        out_shape=jax.ShapeDtypeStruct(
            (shares, devices * steps // shares, out_weight.shape[1]), jnp.bfloat16
        ),
        in_specs=[SMEM] + [VMEM] * 3,
        out_specs=VMEM,
        compiler_params=params,
        name="project",
    )(plan, everyone, lax.ppermute(everyone, "inst", core_pairs), near(out_weight))
    shared = lax.all_to_all(share, "tp", 0, 0, tiled=True)
    return pl.pallas_call(
        add_kernel,
        out_shape=jax.ShapeDtypeStruct(
            (devices // shares, steps, out_weight.shape[1]), jnp.bfloat16
        ),
        in_specs=[VMEM],
        out_specs=VMEM,
        compiler_params=params,
        name="add",
    )(shared)


def solution(mesh):
    in_specs = (
        P("inst", None, "tp"),
        P("inst", None, "tp"),
        P("inst", None, "tp"),
        P("inst", None, "tp"),
        P("inst", None, "tp"),
        P("inst"),
        P("inst"),
        P(),
        P("tp", "inst"),
    )
    out_specs = P("tp", None, "inst")
    return jax.shard_map(body, mesh=mesh, in_specs=in_specs, out_specs=out_specs, check_vma=False)
```

time: 230 us -> 51.3 us (0.22)
  the two profiles are of different devices: /device:TPU:2 before, /device:TPU:1 now
where the time goes in v1:
time: 51.3 us; the launch traced here: 51.2 us
  blocking collectives  37.8 us (74%)
  starting transfers between devices  6.24 us (12%)
  Pallas kernels  4.68 us (9%)
  waiting for transfers between devices  2.22 us (4%)
    all_to_all x2, blocking collectives, over_chips(): lax.all_to_all(x, 'inst', 0, 0, tiled=True, axis_index_groups=same_core)  22.6 us
    all_to_all x1, blocking collectives, body(): shared = lax.all_to_all(share, 'tp', 0, 0, tiled=True)  15.2 us
    ppermute x1, starting transfers between devices, body(): lax.ppermute(queries, 'inst', core_pairs)  3.24 us
    ppermute x1, starting transfers between devices, body(): lax.ppermute(everyone, 'inst', core_pairs)  3 us
    pallas_call x1, Pallas kernels, body(): pl.pallas_call(attend_kernel, out_shape=jax.ShapeDtypeStruct((steps, sent...  2.49 us
    ppermute x1, waiting for transfers between devices, body(): lax.ppermute(everyone, 'inst', core_pairs)  1.19 us
    ppermute x1, waiting for transfers between devices, body(): lax.ppermute(queries, 'inst', core_pairs)  1.04 us
  transfers between devices with their start and end apart: 2, of which 2 were waited for; matrix products, arithmetic and copies ran while one was open for 0% of the time, Pallas kernels for 0%

profile of v1, /device:TPU:1, one launch (start us, length us, event | category | flops | bytes accessed | tf_op | source)
XLA Modules:
  0.0 51.2 jit_solution(7944286695340131725)
XLA Ops:
  0.0 3.2 %collective-permute-start = (bf16[1,4,1024]{2,1,0:T(4,128)(2,1)}, bf16[1,4,1024]{2,1,0:T(4,128)(2,1)S(1)}, u32[]{:S(2)}, u32[]{:S(2)}) collective-permute-start(bf16[1,4,1024]{2,1,0:T(4,128)(2,1)} %query_hbm.1), channel_id=1, source_target_pairs={{0,8},{8,0},{16,24},{24,16},{32,40},{40,32},{48,56},{56,48},{64,72... | collective-permute-start | bytes 24584 | tf_op jit(solution)/shard_map/ppermute | solution.py:306
  3.2 1.0 %collective-permute-done.other_ref = bf16[1,4,1024]{2,1,0:T(4,128)(2,1)S(1)} collective-permute-done((bf16[1,4,1024]{2,1,0:T(4,128)(2,1)}, bf16[1,4,1024]{2,1,0:T(4,128)(2,1)S(1)}, u32[]{:S(2)}, u32[]{:S(2)}) %collective-permute-start) | collective-permute-done | bytes 8224 | tf_op jit(solution)/shard_map/ppermute | solution.py:306
  4.3 0.0 copy-start
  4.3 0.0 copy-start.1
  4.3 1.0 %spread.1 = (bf16[16,4,1024]{2,1,0:T(4,128)(2,1)S(1)}, bf16[4,1024]{1,0:T(4,128)(2,1)S(1)}, bf16[4,128]{1,0:T(4,128)(2,1)S(1)}, bf16[4,128]{1,0:T(4,128)(2,1)S(1)}, s32[18]{0:T(128)S(4)}) custom-call(s32[1]{0:T(128)} %bitcast.me_ref, s32[8]{0:T(128)} %rows_hbm.1, s32[8]{0:T(128)} %blocks_hbm.1, s32[32]{0:T(128)} %lengths_hbm.1, ...), custom_call_target="tpu_custom_call" | custom-call | flops 40000000000 | bytes 60000000 | tf_op jit(solution)/shard_map/spread/pallas_call | solution.py:281
  5.3 11.8 %all_to_all.15.asked_ref = bf16[16,4,1024]{2,1,0:T(4,128)(2,1)S(1)} all-to-all(bf16[16,4,1024]{2,1,0:T(4,128)(2,1)S(1)} %get-tuple-element.11), channel_id=1, replica_groups={{0,16,32,48,64,80,96,112,128,144,160,176,192,208,224,240},{8,24,40,56,7..., dimensions={0} | all-to-all | bytes 262144 | tf_op jit(solution)/shard_map/all_to_all | solution.py:279
  17.1 0.0 copy-done
  17.1 0.0 copy-done.1
  17.1 0.0 copy-start.2
  17.1 2.5 %attend.1 = bf16[4,2176]{1,0:T(4,128)(2,1)S(1)} custom-call(s32[18]{0:T(128)S(4)} %get-tuple-element.10.plan_ref, bf16[16,4,1024]{2,1,0:T(4,128)(2,1)S(1)} %all_to_all.15.asked_ref, bf16[4,1024]{1,0:T(4,128)(2,1)S(1)} %get-tuple-element.12.query_ref, bf16[4,128]{1,0:T(4,128)(2,1)S(1)} %get-tuple-element.13.new_key_ref, ...), custom_call_target="tpu_custom_call" | custom-call | flops 300000000 | bytes 9000000 | tf_op jit(solution)/shard_map/attend/pallas_call | solution.py:311
  19.6 0.1 broadcast_in_dim.2
  19.7 10.8 %all_to_all.16 = bf16[16,4,2176]{2,1,0:T(4,128)(2,1)S(1)} all-to-all(bf16[16,4,2176]{2,1,0:T(4,128)(2,1)S(1)} %broadcast_in_dim.2), channel_id=1, replica_groups={{0,16,32,48,64,80,96,112,128,144,160,176,192,208,224,240},{8,24,40,56,7..., dimensions={0} | all-to-all | bytes 557056 | tf_op jit(solution)/shard_map/all_to_all | solution.py:279
  30.5 0.1 reshape.8.mine_ref
  30.6 3.0 %collective-permute-start.1 = (bf16[64,2176]{1,0:T(8,128)(2,1)S(1)}, bf16[64,2176]{1,0:T(8,128)(2,1)S(1)}, u32[]{:S(2)}, u32[]{:S(2)}) collective-permute-start(bf16[64,2176]{1,0:T(8,128)(2,1)S(1)} %reshape.8.mine_ref), channel_id=1, source_target_pairs={{0,8},{8,0},{16,24},{24,16},{32,40},{40,32},{48,56},{56,48},{64,72... | collective-permute-start | bytes 835592 | tf_op jit(solution)/shard_map/ppermute | solution.py:345
  33.6 1.2 %collective-permute-done.1.other_ref = bf16[64,2176]{1,0:T(8,128)(2,1)S(1)} collective-permute-done((bf16[64,2176]{1,0:T(8,128)(2,1)S(1)}, bf16[64,2176]{1,0:T(8,128)(2,1)S(1)}, u32[]{:S(2)}, u32[]{:S(2)}) %collective-permute-start.1) | collective-permute-done | bytes 278560 | tf_op jit(solution)/shard_map/ppermute | solution.py:345
  34.8 0.0 copy-done.2
  34.8 0.6 %project.1 = bf16[8,16,256]{2,1,0:T(8,128)(2,1)S(1)} custom-call(s32[18]{0:T(128)S(4)} %get-tuple-element.10.plan_ref, bf16[64,2176]{1,0:T(8,128)(2,1)S(1)} %reshape.8.mine_ref, bf16[64,2176]{1,0:T(8,128)(2,1)S(1)} %collective-permute-done.1.other_ref, bf16[1024,256]{1,0:T(8,128)(2,1)S(1)} %copy-done.2), custom_call_target="tpu_custom_call" | custom-call | tf_op jit(solution)/shard_map/project/pallas_call | solution.py:336
  35.3 15.2 %all_to_all.17.shares_ref = bf16[8,16,256]{2,1,0:T(8,128)(2,1)S(1)} all-to-all(bf16[8,16,256]{2,1,0:T(8,128)(2,1)S(1)} %project.1), channel_id=1, replica_groups=mesh['inst'=32,'tp'=8] {'tp'}, dimensions={0} | all-to-all | bytes 131072 | tf_op jit(solution)/shard_map/all_to_all | solution.py:346
  50.5 0.6 %add.1 = bf16[4,4,256]{2,1,0:T(4,128)(2,1)} custom-call(bf16[8,16,256]{2,1,0:T(8,128)(2,1)S(1)} %all_to_all.17.shares_ref), custom_call_target="tpu_custom_call" | custom-call | tf_op jit(solution)/shard_map/add/pallas_call | solution.py:347
Async XLA Ops:
  0.0 4.3 %collective-permute-start = (bf16[1,4,1024]{2,1,0:T(4,128)(2,1)}, bf16[1,4,1024]{2,1,0:T(4,128)(2,1)S(1)}, u32[]{:S(2)}, u32[]{:S(2)}) collective-permute-start(bf16[1,4,1024]{2,1,0:T(4,128)(2,1)} %query_hbm.1), channel_id=1, source_target_pairs={{0,8},{8,0},{16,24},{24,16},{32,40},{40,32},{48,56},{56,48},{64,72... | collective-permute-start | bytes 24584 | tf_op jit(solution)/shard_map/ppermute | solution.py:306
  4.3 12.8 %copy-start = (bf16[8,2048,128]{2,1,0:T(8,128)(2,1)S(1)}, bf16[8,2048,128]{2,1,0:T(8,128)(2,1)}, u32[]{:S(2)}) copy-start(bf16[8,2048,128]{2,1,0:T(8,128)(2,1)} %key_ref.1) | copy-start | bytes 12582916
  4.3 12.8 %copy-start.1 = (bf16[8,2048,128]{2,1,0:T(8,128)(2,1)S(1)}, bf16[8,2048,128]{2,1,0:T(8,128)(2,1)}, u32[]{:S(2)}) copy-start(bf16[8,2048,128]{2,1,0:T(8,128)(2,1)} %value_ref.1) | copy-start | bytes 12582916
  17.1 17.7 %copy-start.2 = (bf16[1024,256]{1,0:T(8,128)(2,1)S(1)}, bf16[1024,256]{1,0:T(8,128)(2,1)}, u32[]{:S(2)}) copy-start(bf16[1024,256]{1,0:T(8,128)(2,1)} %weight_ref.1) | copy-start | bytes 1572868
  30.6 4.2 %collective-permute-start.1 = (bf16[64,2176]{1,0:T(8,128)(2,1)S(1)}, bf16[64,2176]{1,0:T(8,128)(2,1)S(1)}, u32[]{:S(2)}, u32[]{:S(2)}) collective-permute-start(bf16[64,2176]{1,0:T(8,128)(2,1)S(1)} %reshape.8.mine_ref), channel_id=1, source_target_pairs={{0,8},{8,0},{16,24},{24,16},{32,40},{40,32},{48,56},{56,48},{64,72... | collective-permute-start | bytes 835592 | tf_op jit(solution)/shard_map/ppermute | solution.py:345

commit v2 on v1

--- a/solution.py
+++ b/solution.py
@@ -40,7 +40,7 @@
     return jnp.concatenate([q[:, h * HD : (h + 1) * HD] for h in range(HQ)], axis=0)
 
 
-def spread_kernel(
+def plan_kernel(
     block_len,
     me_ref,
     rows_hbm,
@@ -49,18 +49,20 @@
     query_hbm,
     new_key_hbm,
     new_value_hbm,
-    other_ref,
-    spread_ref,
     query_ref,
-    new_key_ref,
-    new_value_ref,
+    fresh_ref,
+    picks_ref,
     plan_ref,
     rows_ref,
     blocks_ref,
     lengths_ref,
+    new_key_ref,
+    new_value_ref,
     sems,
 ):
     slots = rows_ref.shape[0]
+    steps = query_ref.shape[0]
+    heads = HQ * steps
     copies = [
         pltpu.make_async_copy(source, target, sems.at[k])
         for k, (source, target) in enumerate(
@@ -76,16 +78,17 @@
     ]
     for copy in copies:
         copy.start()
+
+    lane = lax.broadcasted_iota(jnp.int32, (HD, WIDTH), 0)
+    chosen = lane % HQ == lax.broadcasted_iota(jnp.int32, (HD, WIDTH), 1) // HD
+    split = PIECES * HQ
+    picks_ref[0] = jnp.where(chosen & (lane < split), 1.0, 0.0).astype(jnp.bfloat16)
+    picks_ref[1] = jnp.where(chosen & (lane >= split), 1.0, 0.0).astype(jnp.bfloat16)
+
     for copy in copies:
         copy.wait()
     me = me_ref[0]
     longest = longest_row(lengths_ref)
-    asked = jnp.where(
-        me // CORES * CORES + (CORES - 1 - me % CORES) == longest,
-        other_ref[0].astype(jnp.float32),
-        query_ref[...].astype(jnp.float32),
-    ).astype(jnp.bfloat16)
-    spread_ref[...] = jnp.broadcast_to(asked[None], spread_ref.shape)
     plan_ref[0] = longest
     plan_ref[1] = me
     for s in range(slots):
@@ -95,13 +98,43 @@
         plan_ref[2 + s] = in_long.astype(jnp.int32)
         plan_ref[2 + slots + s] = jnp.where(in_long | (row == me), valid, 0)
 
+    query = rows_of_heads(query_ref[...].astype(jnp.float32))
+    step_of = lax.broadcasted_iota(jnp.int32, (heads, 1), 0) % steps
+    fresh = []
+    for u in range(steps):
+        score = jnp.sum(
+            query * new_key_ref[u : u + 1, :].astype(jnp.float32), axis=1, keepdims=True
+        )
+        fresh.append(jnp.where(step_of >= u, score, NEG))
+    top = functools.reduce(jnp.maximum, fresh)
+    total = jnp.zeros_like(top)
+    acc = jnp.zeros((heads, HD), jnp.float32)
+    for u in range(steps):
+        weight = jnp.exp2((fresh[u] - top) * C)
+        total += weight
+        acc += weight.astype(jnp.bfloat16).astype(jnp.float32) * new_value_ref[
+            u : u + 1, :
+        ].astype(jnp.float32)
+    fresh_ref[0] = jnp.broadcast_to(top, (heads, HD))
+    fresh_ref[1] = jnp.broadcast_to(total, (heads, HD))
+    fresh_ref[2] = acc
+
+
+def spread_kernel(plan_ref, query_ref, other_ref, spread_ref):
+    me = plan_ref[1]
+    asked = jnp.where(
+        me + 1 - 2 * (me % CORES) == plan_ref[0],
+        other_ref[0].astype(jnp.float32),
+        query_ref[...].astype(jnp.float32),
+    ).astype(jnp.bfloat16)
+    spread_ref[...] = jnp.broadcast_to(asked[None], spread_ref.shape)
+
 
 def attend_kernel(
     plan_ref,
     asked_ref,
     query_ref,
-    new_key_ref,
-    new_value_ref,
+    fresh_ref,
     key_ref,
     value_ref,
     out_ref,
@@ -113,8 +146,7 @@
     heads = HQ * steps
     longest = plan_ref[0]
     mine = plan_ref[1] == longest
-    own_query = rows_of_heads(query_ref[...].astype(jnp.float32))
-    queries[0] = own_query.astype(jnp.bfloat16)
+    queries[0] = rows_of_heads(query_ref[...].astype(jnp.float32)).astype(jnp.bfloat16)
     queries[1] = rows_of_heads(asked_ref[longest // CORES].astype(jnp.float32)).astype(jnp.bfloat16)
 
     column = lax.broadcasted_iota(jnp.int32, (heads, block_len), 1)
@@ -130,23 +162,7 @@
         scores[s] = score
         tops.append(jnp.maximum(jnp.max(score, axis=1, keepdims=True), FLOOR))
 
-    step_of = lax.broadcasted_iota(jnp.int32, (heads, 1), 0) % steps
-    fresh = []
-    for u in range(steps):
-        score = jnp.sum(
-            own_query * new_key_ref[u : u + 1, :].astype(jnp.float32), axis=1, keepdims=True
-        )
-        fresh.append(jnp.where(step_of >= u, score, NEG))
-    top = functools.reduce(jnp.maximum, fresh)
-    total = jnp.zeros_like(top)
-    acc = jnp.zeros((heads, HD), jnp.float32)
-    for u in range(steps):
-        weight = jnp.exp2((fresh[u] - top) * C)
-        total += weight
-        acc += weight.astype(jnp.bfloat16).astype(jnp.float32) * new_value_ref[
-            u : u + 1, :
-        ].astype(jnp.float32)
-    parts = [(mine, top, total, acc)]
+    parts = [(mine, fresh_ref[0][:, :1], fresh_ref[1][:, :1], fresh_ref[2])]
 
     for s in range(slots):
         weights = jnp.exp2((scores[s] - tops[s]) * C)
@@ -181,23 +197,18 @@
             packed = jnp.where(lane == k * HQ + h, piece[rows], packed)
     heads_of = lambda x: [x[h * steps : (h + 1) * steps] for h in range(HQ)]
     sent = jnp.concatenate(heads_of(attended) + heads_of(long_acc) + [packed], axis=1)
-    out_ref[...] = sent.astype(jnp.bfloat16)
-
-
-def project_kernel(steps, plan_ref, mine_ref, other_ref, weight_ref, out_ref):
+    out_ref[...] = jnp.broadcast_to(sent.astype(jnp.bfloat16)[None], out_ref.shape)
+
+
+def project_kernel(steps, plan_ref, picks_ref, mine_ref, other_ref, weight_ref, out_ref):
     half, _ = mine_ref.shape
     rows = CORES * half
     longest = plan_ref[0]
     first = plan_ref[1] % CORES == 0
     both = lambda cols: jnp.concatenate([mine_ref[:, cols], other_ref[:, cols]], axis=0)
     stats = both(slice(2 * WIDTH, 2 * WIDTH + HD))
-    lane = lax.broadcasted_iota(jnp.int32, (HD, WIDTH), 0)
-    chosen = lane % HQ == lax.broadcasted_iota(jnp.int32, (HD, WIDTH), 1) // HD
-    split = PIECES * HQ
-    pick_top = jnp.where(chosen & (lane < split), 1.0, 0.0).astype(jnp.bfloat16)
-    pick_sum = jnp.where(chosen & (lane >= split), 1.0, 0.0).astype(jnp.bfloat16)
-    tops = jnp.dot(stats, pick_top, preferred_element_type=jnp.float32)
-    sums = jnp.dot(stats, pick_sum, preferred_element_type=jnp.float32)
+    tops = jnp.dot(stats, picks_ref[0], preferred_element_type=jnp.float32)
+    sums = jnp.dot(stats, picks_ref[1], preferred_element_type=jnp.float32)
     accs = both(slice(WIDTH, 2 * WIDTH)).astype(jnp.float32)
 
     pair = 2 * steps
@@ -278,40 +289,48 @@
     def over_chips(x):
         return lax.all_to_all(x, "inst", 0, 0, tiled=True, axis_index_groups=same_core)
 
-    spread, query, new_key, new_value, plan = pl.pallas_call(
-        functools.partial(spread_kernel, block_len),
+    other = lax.ppermute(queries, "inst", core_pairs)
+    query, fresh, picks, plan = pl.pallas_call(
+        functools.partial(plan_kernel, block_len),
         out_shape=[
-            pltpu.VMEM((chips, steps, width), jnp.bfloat16),
             pltpu.VMEM((steps, width), jnp.bfloat16),
-            pltpu.VMEM((steps, HD), jnp.bfloat16),
-            pltpu.VMEM((steps, HD), jnp.bfloat16),
+            pltpu.VMEM((3, heads, HD), jnp.float32),
+            pltpu.VMEM((2, HD, width), jnp.bfloat16),
             pltpu.SMEM((2 + 2 * slots,), jnp.int32),
         ],
-        in_specs=[SMEM] + [HBM] * 6 + [VMEM],
-        out_specs=[VMEM] * 4 + [SMEM],
+        in_specs=[SMEM] + [HBM] * 6,
+        out_specs=[VMEM] * 3 + [SMEM],
         scratch_shapes=[
             pltpu.SMEM((slots,), jnp.int32),
             pltpu.SMEM((slots,), jnp.int32),
             pltpu.SMEM(lengths.shape, jnp.int32),
+            pltpu.VMEM((steps, HD), jnp.bfloat16),
+            pltpu.VMEM((steps, HD), jnp.bfloat16),
             pltpu.SemaphoreType.DMA((6,)),
         ],
+        compiler_params=params,
+        cost_estimate=pl.CostEstimate(flops=1_000_000, bytes_accessed=3_000_000, transcendentals=0),
+        name="plan",
+    )(me, *map(far, (slot_rows, slot_blocks, lengths, queries, new_keys, new_values)))
+    plan = pltpu.with_memory_space_constraint(plan, pltpu.SMEM)
+    picks = near(picks)
+    spread = pl.pallas_call(
+        spread_kernel,
+        out_shape=pltpu.VMEM((chips, steps, width), jnp.bfloat16),
+        in_specs=[SMEM, VMEM, VMEM],
+        out_specs=VMEM,
         compiler_params=params,
         cost_estimate=pl.CostEstimate(
             flops=40_000_000_000, bytes_accessed=60_000_000, transcendentals=0
         ),
         name="spread",
-    )(
-        me,
-        *map(far, (slot_rows, slot_blocks, lengths, queries, new_keys, new_values)),
-        lax.ppermute(queries, "inst", core_pairs),
-    )
-    plan = pltpu.with_memory_space_constraint(plan, pltpu.SMEM)
+    )(plan, near(query), other)
     asked = over_chips(spread)
     sent_cols = 2 * width + HD
     partial = pl.pallas_call(
         attend_kernel,
-        out_shape=jax.ShapeDtypeStruct((steps, sent_cols), jnp.bfloat16),
-        in_specs=[SMEM] + [VMEM] * 6,
+        out_shape=pltpu.VMEM((chips, steps, sent_cols), jnp.bfloat16),
+        in_specs=[SMEM] + [VMEM] * 5,
         out_specs=VMEM,
         scratch_shapes=[
             pltpu.VMEM((2, heads, HD), jnp.bfloat16),
@@ -322,27 +341,19 @@
             flops=300_000_000, bytes_accessed=9_000_000, transcendentals=600_000
         ),
         name="attend",
-    )(
-        plan,
-        asked,
-        near(query),
-        near(new_key),
-        near(new_value),
-        near(key_blocks),
-        near(value_blocks),
-    )
-    everyone = over_chips(jnp.broadcast_to(partial[None], (chips, steps, sent_cols)))
+    )(plan, asked, near(query), near(fresh), near(key_blocks), near(value_blocks))
+    everyone = over_chips(partial)
     everyone = everyone.reshape(chips * steps, sent_cols)
     share = pl.pallas_call(
         functools.partial(project_kernel, steps),
         out_shape=jax.ShapeDtypeStruct(
             (shares, devices * steps // shares, out_weight.shape[1]), jnp.bfloat16
         ),
-        in_specs=[SMEM] + [VMEM] * 3,
+        in_specs=[SMEM] + [VMEM] * 4,
         out_specs=VMEM,
         compiler_params=params,
         name="project",
-    )(plan, everyone, lax.ppermute(everyone, "inst", core_pairs), near(out_weight))
+    )(plan, picks, everyone, lax.ppermute(everyone, "inst", core_pairs), near(out_weight))
     shared = lax.all_to_all(share, "tp", 0, 0, tiled=True)
     return pl.pallas_call(
         add_kernel,

time: 51.3 us -> 50.2 us (0.979)
  waiting for transfers between devices: 2.22 us -> 1.23 us
    ppermute x1, waiting for transfers between devices: 1.04 us -> 0.05 us  [body(): other = lax.ppermute(queries, 'inst', core_pairs)]
    pallas_call x2 -> x3, Pallas kernels: 3.5 us -> 3.4 us  [the longest x1 2.4 us: body(): pl.pallas_call(attend_kernel, out_shape=pltpu.VMEM((chips, steps, sent_co...]
  transfers between devices with their start and end apart: 2 -> 2, of which waited for: 2 -> 1; matrix products, arithmetic and copies ran while one was open for 0% -> 0% of each run, Pallas kernels for 0% -> 2%
where the time goes in v2:
time: 50.2 us; the launch traced here: 50 us
  blocking collectives  37.8 us (75%)
  starting transfers between devices  6.24 us (12%)
  Pallas kernels  4.59 us (9%)
  waiting for transfers between devices  1.23 us (2%)
    all_to_all x2, blocking collectives, over_chips(): lax.all_to_all(x, 'inst', 0, 0, tiled=True, axis_index_groups=same_core)  22.6 us
    all_to_all x1, blocking collectives, body(): shared = lax.all_to_all(share, 'tp', 0, 0, tiled=True)  15.2 us
    ppermute x1, starting transfers between devices, body(): other = lax.ppermute(queries, 'inst', core_pairs)  3.24 us
    ppermute x1, starting transfers between devices, body(): lax.ppermute(everyone, 'inst', core_pairs)  3 us
    pallas_call x1, Pallas kernels, body(): pl.pallas_call(attend_kernel, out_shape=pltpu.VMEM((chips, steps, sent_co...  2.4 us
    ppermute x1, waiting for transfers between devices, body(): lax.ppermute(everyone, 'inst', core_pairs)  1.19 us
  transfers between devices with their start and end apart: 2, of which 1 were waited for; matrix products, arithmetic and copies ran while one was open for 0% of the time, Pallas kernels for 2%

profile of v2, /device:TPU:1, one launch (start us, length us, event | category | flops | bytes accessed | tf_op | source)
XLA Modules:
  0.0 50.0 jit_solution(520300253946815024)
XLA Ops:
  0.0 3.2 %collective-permute-start = (bf16[1,4,1024]{2,1,0:T(4,128)(2,1)}, bf16[1,4,1024]{2,1,0:T(4,128)(2,1)S(1)}, u32[]{:S(2)}, u32[]{:S(2)}) collective-permute-start(bf16[1,4,1024]{2,1,0:T(4,128)(2,1)} %query_hbm.1), channel_id=1, source_target_pairs={{0,8},{8,0},{16,24},{24,16},{32,40},{40,32},{48,56},{56,48},{64,72... | collective-permute-start | bytes 24584 | tf_op jit(solution)/shard_map/ppermute | solution.py:292
  3.2 1.0 %plan.1 = (bf16[4,1024]{1,0:T(4,128)(2,1)S(1)}, f32[3,32,128]{2,1,0:T(8,128)S(1)}, bf16[2,128,1024]{2,1,0:T(8,128)(2,1)S(1)}, s32[18]{0:T(128)S(4)}) custom-call(s32[1]{0:T(128)} %bitcast.me_ref, s32[8]{0:T(128)} %rows_hbm.1, s32[8]{0:T(128)} %blocks_hbm.1, s32[32]{0:T(128)} %lengths_hbm.1, bf16[1,4,1024]{2,1,0:T(4,128)(2,1)} %query_hbm.1, ...), custom_call_target="tpu_custom_call" | custom-call | flops 1000000 | bytes 3000000 | tf_op jit(solution)/shard_map/plan/pallas_call | solution.py:293
  4.2 0.0 collective-permute-done.other_ref
  4.3 0.0 copy-start
  4.3 0.0 copy-start.1
  4.3 11.8 %all_to_all.15.asked_ref = bf16[16,4,1024]{2,1,0:T(4,128)(2,1)S(1)} all-to-all(bf16[16,4,1024]{2,1,0:T(4,128)(2,1)S(1)} %spread.1), channel_id=1, replica_groups={{0,16,32,48,64,80,96,112,128,144,160,176,192,208,224,240},{8,24,40,56,7..., dimensions={0} | all-to-all | bytes 262144 | tf_op jit(solution)/shard_map/all_to_all | solution.py:290
  16.1 0.0 copy-done
  16.1 0.0 copy-done.1
  16.1 0.0 copy-start.2
  16.1 2.4 %attend.1 = bf16[16,4,2176]{2,1,0:T(4,128)(2,1)S(1)} custom-call(s32[18]{0:T(128)S(4)} %get-tuple-element.9.plan_ref, bf16[16,4,1024]{2,1,0:T(4,128)(2,1)S(1)} %all_to_all.15.asked_ref, bf16[4,1024]{1,0:T(4,128)(2,1)S(1)} %get-tuple-element.11.query_ref, f32[3,32,128]{2,1,0:T(8,128)S(1)} %get-tuple-element.12.fresh_ref, bf16[8,2048,128]{2,1,0:T(8,128)(2,1)S(1)} %copy-done, ...), custom_call_target="tpu_custom_call" | custom-call | flops 300000000 | bytes 9000000 | tf_op jit(solution)/shard_map/attend/pallas_call | solution.py:330
  18.5 10.8 %all_to_all.16 = bf16[16,4,2176]{2,1,0:T(4,128)(2,1)S(1)} all-to-all(bf16[16,4,2176]{2,1,0:T(4,128)(2,1)S(1)} %attend.1), channel_id=1, replica_groups={{0,16,32,48,64,80,96,112,128,144,160,176,192,208,224,240},{8,24,40,56,7..., dimensions={0} | all-to-all | bytes 557056 | tf_op jit(solution)/shard_map/all_to_all | solution.py:290
  29.3 0.1 reshape.7.mine_ref
  29.4 3.0 %collective-permute-start.1 = (bf16[64,2176]{1,0:T(8,128)(2,1)S(1)}, bf16[64,2176]{1,0:T(8,128)(2,1)S(1)}, u32[]{:S(2)}, u32[]{:S(2)}) collective-permute-start(bf16[64,2176]{1,0:T(8,128)(2,1)S(1)} %reshape.7.mine_ref), channel_id=1, source_target_pairs={{0,8},{8,0},{16,24},{24,16},{32,40},{40,32},{48,56},{56,48},{64,72... | collective-permute-start | bytes 835592 | tf_op jit(solution)/shard_map/ppermute | solution.py:356
  32.4 1.2 %collective-permute-done.1.other_ref = bf16[64,2176]{1,0:T(8,128)(2,1)S(1)} collective-permute-done((bf16[64,2176]{1,0:T(8,128)(2,1)S(1)}, bf16[64,2176]{1,0:T(8,128)(2,1)S(1)}, u32[]{:S(2)}, u32[]{:S(2)}) %collective-permute-start.1) | collective-permute-done | bytes 278560 | tf_op jit(solution)/shard_map/ppermute | solution.py:356
  33.6 0.0 copy-done.2
  33.6 0.6 %project.1 = bf16[8,16,256]{2,1,0:T(8,128)(2,1)S(1)} custom-call(s32[18]{0:T(128)S(4)} %get-tuple-element.9.plan_ref, bf16[2,128,1024]{2,1,0:T(8,128)(2,1)S(1)} %get-tuple-element.10.picks_ref, bf16[64,2176]{1,0:T(8,128)(2,1)S(1)} %reshape.7.mine_ref, bf16[64,2176]{1,0:T(8,128)(2,1)S(1)} %collective-permute-done.1.other_ref, bf16[1024,256]{1,0:T(8,128)(2,1)S(1)} %copy-done.2), custom_call_target="tpu_custom_call" | custom-call | tf_op jit(solution)/shard_map/project/pallas_call | solution.py:347
  34.2 15.2 %all_to_all.17.shares_ref = bf16[8,16,256]{2,1,0:T(8,128)(2,1)S(1)} all-to-all(bf16[8,16,256]{2,1,0:T(8,128)(2,1)S(1)} %project.1), channel_id=1, replica_groups=mesh['inst'=32,'tp'=8] {'tp'}, dimensions={0} | all-to-all | bytes 131072 | tf_op jit(solution)/shard_map/all_to_all | solution.py:357
  49.4 0.6 %add.1 = bf16[4,4,256]{2,1,0:T(4,128)(2,1)} custom-call(bf16[8,16,256]{2,1,0:T(8,128)(2,1)S(1)} %all_to_all.17.shares_ref), custom_call_target="tpu_custom_call" | custom-call | tf_op jit(solution)/shard_map/add/pallas_call | solution.py:358
  (1 shorter events, 0.0 us)
Async XLA Ops:
  0.0 4.3 %collective-permute-start = (bf16[1,4,1024]{2,1,0:T(4,128)(2,1)}, bf16[1,4,1024]{2,1,0:T(4,128)(2,1)S(1)}, u32[]{:S(2)}, u32[]{:S(2)}) collective-permute-start(bf16[1,4,1024]{2,1,0:T(4,128)(2,1)} %query_hbm.1), channel_id=1, source_target_pairs={{0,8},{8,0},{16,24},{24,16},{32,40},{40,32},{48,56},{56,48},{64,72... | collective-permute-start | bytes 24584 | tf_op jit(solution)/shard_map/ppermute | solution.py:292
  4.3 11.8 %copy-start = (bf16[8,2048,128]{2,1,0:T(8,128)(2,1)S(1)}, bf16[8,2048,128]{2,1,0:T(8,128)(2,1)}, u32[]{:S(2)}) copy-start(bf16[8,2048,128]{2,1,0:T(8,128)(2,1)} %key_ref.1) | copy-start | bytes 12582916
  4.3 11.8 %copy-start.1 = (bf16[8,2048,128]{2,1,0:T(8,128)(2,1)S(1)}, bf16[8,2048,128]{2,1,0:T(8,128)(2,1)}, u32[]{:S(2)}) copy-start(bf16[8,2048,128]{2,1,0:T(8,128)(2,1)} %value_ref.1) | copy-start | bytes 12582916
  16.1 17.5 %copy-start.2 = (bf16[1024,256]{1,0:T(8,128)(2,1)S(1)}, bf16[1024,256]{1,0:T(8,128)(2,1)}, u32[]{:S(2)}) copy-start(bf16[1024,256]{1,0:T(8,128)(2,1)} %weight_ref.1) | copy-start | bytes 1572868
  29.4 4.2 %collective-permute-start.1 = (bf16[64,2176]{1,0:T(8,128)(2,1)S(1)}, bf16[64,2176]{1,0:T(8,128)(2,1)S(1)}, u32[]{:S(2)}, u32[]{:S(2)}) collective-permute-start(bf16[64,2176]{1,0:T(8,128)(2,1)S(1)} %reshape.7.mine_ref), channel_id=1, source_target_pairs={{0,8},{8,0},{16,24},{24,16},{32,40},{40,32},{48,56},{56,48},{64,72... | collective-permute-start | bytes 835592 | tf_op jit(solution)/shard_map/ppermute | solution.py:356

commit v3 on v2

--- a/solution.py
+++ b/solution.py
@@ -16,6 +16,8 @@
 C = HD ** (-0.5) / math.log(2.0)
 PIECES = 3
 CORES = 2
+CHIP_ORDER = [2, 14, 12, 9, 0, 3, 4, 10, 11, 5, 15, 8, 13, 7, 6, 1]
+TP_ORDER = [0, 2, 4, 6, 1, 3, 5, 7]
 
 
 def longest_row(lengths_ref):
@@ -91,6 +93,10 @@
     longest = longest_row(lengths_ref)
     plan_ref[0] = longest
     plan_ref[1] = me
+    place = jnp.int32(0)
+    for k, chip in enumerate(CHIP_ORDER):
+        place = jnp.where(longest // CORES == chip, k, place)
+    plan_ref[2 + 2 * slots] = place
     for s in range(slots):
         row = rows_ref[s]
         in_long = row == longest
@@ -147,7 +153,7 @@
     longest = plan_ref[0]
     mine = plan_ref[1] == longest
     queries[0] = rows_of_heads(query_ref[...].astype(jnp.float32)).astype(jnp.bfloat16)
-    queries[1] = rows_of_heads(asked_ref[longest // CORES].astype(jnp.float32)).astype(jnp.bfloat16)
+    queries[1] = rows_of_heads(asked_ref[plan_ref[2 + 2 * slots]].astype(jnp.float32)).astype(jnp.bfloat16)
 
     column = lax.broadcasted_iota(jnp.int32, (heads, block_len), 1)
     tops = []
@@ -200,7 +206,7 @@
     out_ref[...] = jnp.broadcast_to(sent.astype(jnp.bfloat16)[None], out_ref.shape)
 
 
-def project_kernel(steps, plan_ref, picks_ref, mine_ref, other_ref, weight_ref, out_ref):
+def project_kernel(steps, place_at, plan_ref, picks_ref, mine_ref, other_ref, weight_ref, out_ref):
     half, _ = mine_ref.shape
     rows = CORES * half
     longest = plan_ref[0]
@@ -226,20 +232,27 @@
     other = other_ref[:, :WIDTH].astype(jnp.float32)
     own, other = jnp.where(first, own, other), jnp.where(first, other, own)
     shape = (half // pair, pair, WIDTH)
-    chip = lax.broadcasted_iota(jnp.int32, shape, 0) * (pair // steps)
-    chip = chip + lax.broadcasted_iota(jnp.int32, shape, 1) // steps
-    attended = [
-        jnp.where(chip * CORES + core == longest, merged[None], fold(part)).reshape(half, WIDTH)
-        for core, part in enumerate((own, other))
-    ]
+    place = lax.broadcasted_iota(jnp.int32, shape, 0) * (pair // steps)
+    place = place + lax.broadcasted_iota(jnp.int32, shape, 1) // steps
+    attended = []
+    for core, part in enumerate((own, other)):
+        wanted = jnp.where(longest % CORES == core, plan_ref[place_at], -1)
+        attended.append(jnp.where(place == wanted, merged[None], fold(part)).reshape(half, WIDTH))
     product = jnp.dot(
         jnp.concatenate(attended, axis=0).astype(jnp.bfloat16),
         weight_ref[...],
         preferred_element_type=jnp.float32,
     )
-    shares, each, cols = out_ref.shape
-    product = product.reshape(CORES, shares, each // CORES, cols)
-    out_ref[...] = jnp.concatenate([product[c] for c in range(CORES)], axis=1).astype(out_ref.dtype)
+    shares, each, _ = out_ref.shape
+    chips = each // (CORES * steps)
+    for k, share in enumerate(TP_ORDER):
+        starts = [
+            core * half + CHIP_ORDER.index(share * chips + chip) * steps
+            for core in range(CORES)
+            for chip in range(chips)
+        ]
+        rows = jnp.concatenate([product[at : at + steps] for at in starts], axis=0)
+        out_ref[k] = rows.astype(out_ref.dtype)
 
 
 def add_kernel(shares_ref, out_ref):
@@ -282,7 +295,7 @@
     chips = devices // CORES
     shares = lax.axis_size("tp")
     me = lax.axis_index("inst").astype(jnp.int32).reshape(1)
-    same_core = [[chip * CORES + core for chip in range(chips)] for core in range(CORES)]
+    same_core = [[chip * CORES + core for chip in CHIP_ORDER] for core in range(CORES)]
     core_pairs = [(i, i ^ 1) for i in range(devices)]
     params = pltpu.CompilerParams(vmem_limit_bytes=24 * 1024 * 1024)
 
@@ -296,7 +309,7 @@
             pltpu.VMEM((steps, width), jnp.bfloat16),
             pltpu.VMEM((3, heads, HD), jnp.float32),
             pltpu.VMEM((2, HD, width), jnp.bfloat16),
-            pltpu.SMEM((2 + 2 * slots,), jnp.int32),
+            pltpu.SMEM((3 + 2 * slots,), jnp.int32),
         ],
         in_specs=[SMEM] + [HBM] * 6,
         out_specs=[VMEM] * 3 + [SMEM],
@@ -345,7 +358,7 @@
     everyone = over_chips(partial)
     everyone = everyone.reshape(chips * steps, sent_cols)
     share = pl.pallas_call(
-        functools.partial(project_kernel, steps),
+        functools.partial(project_kernel, steps, 2 + 2 * slots),
         out_shape=jax.ShapeDtypeStruct(
             (shares, devices * steps // shares, out_weight.shape[1]), jnp.bfloat16
         ),
@@ -354,7 +367,7 @@
         compiler_params=params,
         name="project",
     )(plan, picks, everyone, lax.ppermute(everyone, "inst", core_pairs), near(out_weight))
-    shared = lax.all_to_all(share, "tp", 0, 0, tiled=True)
+    shared = lax.all_to_all(share, "tp", 0, 0, tiled=True, axis_index_groups=[TP_ORDER])
     return pl.pallas_call(
         add_kernel,
         out_shape=jax.ShapeDtypeStruct(

time: 50.2 us -> 47.9 us (0.954)
  blocking collectives: 37.8 us -> 35.5 us
    all_to_all x2, blocking collectives: 22.6 us -> 20.9 us  [over_chips(): lax.all_to_all(x, 'inst', 0, 0, tiled=True, axis_index_groups=same_core)]
    all_to_all x1, blocking collectives: 15.2 us -> 14.6 us  [body(): lax.all_to_all(share, 'tp', 0, 0, tiled=True, axis_index_groups=[TP_ORDER])]
  transfers between devices with their start and end apart: 2 -> 2, of which waited for: 1 -> 2; matrix products, arithmetic and copies ran while one was open for 0% -> 0% of each run, Pallas kernels for 2% -> 2%
where the time goes in v3:
time: 47.9 us; the launch traced here: 47.7 us
  blocking collectives  35.5 us (74%)
  starting transfers between devices  6.25 us (13%)
  Pallas kernels  4.59 us (10%)
  waiting for transfers between devices  1.24 us (3%)
    all_to_all x2, blocking collectives, over_chips(): lax.all_to_all(x, 'inst', 0, 0, tiled=True, axis_index_groups=same_core)  20.9 us
    all_to_all x1, blocking collectives, body(): lax.all_to_all(share, 'tp', 0, 0, tiled=True, axis_index_groups=[TP_ORDER])  14.6 us
    ppermute x1, starting transfers between devices, body(): other = lax.ppermute(queries, 'inst', core_pairs)  3.24 us
    ppermute x1, starting transfers between devices, body(): lax.ppermute(everyone, 'inst', core_pairs)  3.01 us
    pallas_call x1, Pallas kernels, body(): pl.pallas_call(attend_kernel, out_shape=pltpu.VMEM((chips, steps, sent_co...  2.4 us
    ppermute x1, waiting for transfers between devices, body(): lax.ppermute(everyone, 'inst', core_pairs)  1.19 us
    pallas_call x1, Pallas kernels, body(): pl.pallas_call(functools.partial(plan_kernel, block_len), out_shape=[pltp...  0.98 us
  transfers between devices with their start and end apart: 2, of which 2 were waited for; matrix products, arithmetic and copies ran while one was open for 0% of the time, Pallas kernels for 2%

profile of v3, /device:TPU:1, one launch (start us, length us, event | category | flops | bytes accessed | tf_op | source)
XLA Modules:
  0.0 47.7 jit_solution(15463462349392289762)
XLA Ops:
  0.0 3.2 %collective-permute-start = (bf16[1,4,1024]{2,1,0:T(4,128)(2,1)}, bf16[1,4,1024]{2,1,0:T(4,128)(2,1)S(1)}, u32[]{:S(2)}, u32[]{:S(2)}) collective-permute-start(bf16[1,4,1024]{2,1,0:T(4,128)(2,1)} %query_hbm.1), channel_id=1, source_target_pairs={{0,8},{8,0},{16,24},{24,16},{32,40},{40,32},{48,56},{56,48},{64,72... | collective-permute-start | bytes 24584 | tf_op jit(solution)/shard_map/ppermute | solution.py:305
  3.2 1.0 %plan.1 = (bf16[4,1024]{1,0:T(4,128)(2,1)S(1)}, f32[3,32,128]{2,1,0:T(8,128)S(1)}, bf16[2,128,1024]{2,1,0:T(8,128)(2,1)S(1)}, s32[19]{0:T(128)S(4)}) custom-call(s32[1]{0:T(128)} %bitcast.me_ref, s32[8]{0:T(128)} %rows_hbm.1, s32[8]{0:T(128)} %blocks_hbm.1, s32[32]{0:T(128)} %lengths_hbm.1, bf16[1,4,1024]{2,1,0:T(4,128)(2,1)} %query_hbm.1, ...), custom_call_target="tpu_custom_call" | custom-call | flops 1000000 | bytes 3000000 | tf_op jit(solution)/shard_map/plan/pallas_call | solution.py:306
  4.2 0.1 collective-permute-done.other_ref
  4.3 0.0 copy-start
  4.3 0.0 copy-start.1
  4.3 10.7 %all_to_all.15.asked_ref = bf16[16,4,1024]{2,1,0:T(4,128)(2,1)S(1)} all-to-all(bf16[16,4,1024]{2,1,0:T(4,128)(2,1)S(1)} %spread.1), channel_id=1, replica_groups={{32,224,192,144,0,48,64,160,176,80,240,128,208,112,96,16},{40,232,200,1..., dimensions={0} | all-to-all | bytes 262144 | tf_op jit(solution)/shard_map/all_to_all | solution.py:303
  15.0 0.0 copy-done
  15.0 0.0 copy-done.1
  15.0 0.0 copy-start.2
  15.1 2.4 %attend.1 = bf16[16,4,2176]{2,1,0:T(4,128)(2,1)S(1)} custom-call(s32[19]{0:T(128)S(4)} %get-tuple-element.9.plan_ref, bf16[16,4,1024]{2,1,0:T(4,128)(2,1)S(1)} %all_to_all.15.asked_ref, bf16[4,1024]{1,0:T(4,128)(2,1)S(1)} %get-tuple-element.11.query_ref, f32[3,32,128]{2,1,0:T(8,128)S(1)} %get-tuple-element.12.fresh_ref, bf16[8,2048,128]{2,1,0:T(8,128)(2,1)S(1)} %copy-done, ...), custom_call_target="tpu_custom_call" | custom-call | flops 300000000 | bytes 9000000 | tf_op jit(solution)/shard_map/attend/pallas_call | solution.py:343
  17.5 10.2 %all_to_all.16 = bf16[16,4,2176]{2,1,0:T(4,128)(2,1)S(1)} all-to-all(bf16[16,4,2176]{2,1,0:T(4,128)(2,1)S(1)} %attend.1), channel_id=1, replica_groups={{32,224,192,144,0,48,64,160,176,80,240,128,208,112,96,16},{40,232,200,1..., dimensions={0} | all-to-all | bytes 557056 | tf_op jit(solution)/shard_map/all_to_all | solution.py:303
  27.6 0.1 reshape.7.mine_ref
  27.7 3.0 %collective-permute-start.1 = (bf16[64,2176]{1,0:T(8,128)(2,1)S(1)}, bf16[64,2176]{1,0:T(8,128)(2,1)S(1)}, u32[]{:S(2)}, u32[]{:S(2)}) collective-permute-start(bf16[64,2176]{1,0:T(8,128)(2,1)S(1)} %reshape.7.mine_ref), channel_id=1, source_target_pairs={{0,8},{8,0},{16,24},{24,16},{32,40},{40,32},{48,56},{56,48},{64,72... | collective-permute-start | bytes 835592 | tf_op jit(solution)/shard_map/ppermute | solution.py:369
  30.7 1.2 %collective-permute-done.1.other_ref = bf16[64,2176]{1,0:T(8,128)(2,1)S(1)} collective-permute-done((bf16[64,2176]{1,0:T(8,128)(2,1)S(1)}, bf16[64,2176]{1,0:T(8,128)(2,1)S(1)}, u32[]{:S(2)}, u32[]{:S(2)}) %collective-permute-start.1) | collective-permute-done | bytes 278560 | tf_op jit(solution)/shard_map/ppermute | solution.py:369
  31.9 0.0 copy-done.2
  31.9 0.6 %project.1 = bf16[8,16,256]{2,1,0:T(8,128)(2,1)S(1)} custom-call(s32[19]{0:T(128)S(4)} %get-tuple-element.9.plan_ref, bf16[2,128,1024]{2,1,0:T(8,128)(2,1)S(1)} %get-tuple-element.10.picks_ref, bf16[64,2176]{1,0:T(8,128)(2,1)S(1)} %reshape.7.mine_ref, bf16[64,2176]{1,0:T(8,128)(2,1)S(1)} %collective-permute-done.1.other_ref, bf16[1024,256]{1,0:T(8,128)(2,1)S(1)} %copy-done.2), custom_call_target="tpu_custom_call" | custom-call | tf_op jit(solution)/shard_map/project/pallas_call | solution.py:360
  32.5 14.6 %all_to_all.17.shares_ref = bf16[8,16,256]{2,1,0:T(8,128)(2,1)S(1)} all-to-all(bf16[8,16,256]{2,1,0:T(8,128)(2,1)S(1)} %project.1), channel_id=1, replica_groups={{0,2,4,6,1,3,5,7},{8,10,12,14,9,11,13,15},{16,18,20,22,17,19,21,23},{24..., dimensions={0} | all-to-all | bytes 131072 | tf_op jit(solution)/shard_map/all_to_all | solution.py:370
  47.1 0.6 %add.1 = bf16[4,4,256]{2,1,0:T(4,128)(2,1)} custom-call(bf16[8,16,256]{2,1,0:T(8,128)(2,1)S(1)} %all_to_all.17.shares_ref), custom_call_target="tpu_custom_call" | custom-call | tf_op jit(solution)/shard_map/add/pallas_call | solution.py:371
  (1 shorter events, 0.0 us)
Async XLA Ops:
  0.0 4.3 %collective-permute-start = (bf16[1,4,1024]{2,1,0:T(4,128)(2,1)}, bf16[1,4,1024]{2,1,0:T(4,128)(2,1)S(1)}, u32[]{:S(2)}, u32[]{:S(2)}) collective-permute-start(bf16[1,4,1024]{2,1,0:T(4,128)(2,1)} %query_hbm.1), channel_id=1, source_target_pairs={{0,8},{8,0},{16,24},{24,16},{32,40},{40,32},{48,56},{56,48},{64,72... | collective-permute-start | bytes 24584 | tf_op jit(solution)/shard_map/ppermute | solution.py:305
  4.3 10.8 %copy-start = (bf16[8,2048,128]{2,1,0:T(8,128)(2,1)S(1)}, bf16[8,2048,128]{2,1,0:T(8,128)(2,1)}, u32[]{:S(2)}) copy-start(bf16[8,2048,128]{2,1,0:T(8,128)(2,1)} %key_ref.1) | copy-start | bytes 12582916
  4.3 10.8 %copy-start.1 = (bf16[8,2048,128]{2,1,0:T(8,128)(2,1)S(1)}, bf16[8,2048,128]{2,1,0:T(8,128)(2,1)}, u32[]{:S(2)}) copy-start(bf16[8,2048,128]{2,1,0:T(8,128)(2,1)} %value_ref.1) | copy-start | bytes 12582916
  15.0 16.8 %copy-start.2 = (bf16[1024,256]{1,0:T(8,128)(2,1)S(1)}, bf16[1024,256]{1,0:T(8,128)(2,1)}, u32[]{:S(2)}) copy-start(bf16[1024,256]{1,0:T(8,128)(2,1)} %weight_ref.1) | copy-start | bytes 1572868
  27.7 4.2 %collective-permute-start.1 = (bf16[64,2176]{1,0:T(8,128)(2,1)S(1)}, bf16[64,2176]{1,0:T(8,128)(2,1)S(1)}, u32[]{:S(2)}, u32[]{:S(2)}) collective-permute-start(bf16[64,2176]{1,0:T(8,128)(2,1)S(1)} %reshape.7.mine_ref), channel_id=1, source_target_pairs={{0,8},{8,0},{16,24},{24,16},{32,40},{40,32},{48,56},{56,48},{64,72... | collective-permute-start | bytes 835592 | tf_op jit(solution)/shard_map/ppermute | solution.py:369

commit v4 on v3

--- a/solution.py
+++ b/solution.py
@@ -16,8 +16,9 @@
 C = HD ** (-0.5) / math.log(2.0)
 PIECES = 3
 CORES = 2
-CHIP_ORDER = [2, 14, 12, 9, 0, 3, 4, 10, 11, 5, 15, 8, 13, 7, 6, 1]
-TP_ORDER = [0, 2, 4, 6, 1, 3, 5, 7]
+ASK_ORDER = [10, 11, 8, 9, 15, 12, 13, 14, 0, 1, 2, 3, 5, 6, 7, 4]
+SEND_ORDER = [10, 11, 5, 15, 8, 13, 7, 6, 1, 2, 14, 12, 9, 0, 3, 4]
+TP_ORDER = [4, 6, 1, 3, 5, 7, 0, 2]
 
 
 def longest_row(lengths_ref):
@@ -93,10 +94,11 @@
     longest = longest_row(lengths_ref)
     plan_ref[0] = longest
     plan_ref[1] = me
-    place = jnp.int32(0)
-    for k, chip in enumerate(CHIP_ORDER):
-        place = jnp.where(longest // CORES == chip, k, place)
-    plan_ref[2 + 2 * slots] = place
+    for at, order in enumerate((ASK_ORDER, SEND_ORDER)):
+        place = jnp.int32(0)
+        for k, chip in enumerate(order):
+            place = jnp.where(longest // CORES == chip, k, place)
+        plan_ref[2 + 2 * slots + at] = place
     for s in range(slots):
         row = rows_ref[s]
         in_long = row == longest
@@ -247,7 +249,7 @@
     chips = each // (CORES * steps)
     for k, share in enumerate(TP_ORDER):
         starts = [
-            core * half + CHIP_ORDER.index(share * chips + chip) * steps
+            core * half + SEND_ORDER.index(share * chips + chip) * steps
             for core in range(CORES)
             for chip in range(chips)
         ]
@@ -295,11 +297,11 @@
     chips = devices // CORES
     shares = lax.axis_size("tp")
     me = lax.axis_index("inst").astype(jnp.int32).reshape(1)
-    same_core = [[chip * CORES + core for chip in CHIP_ORDER] for core in range(CORES)]
     core_pairs = [(i, i ^ 1) for i in range(devices)]
     params = pltpu.CompilerParams(vmem_limit_bytes=24 * 1024 * 1024)
 
-    def over_chips(x):
+    def over_chips(x, order):
+        same_core = [[chip * CORES + core for chip in order] for core in range(CORES)]
         return lax.all_to_all(x, "inst", 0, 0, tiled=True, axis_index_groups=same_core)
 
     other = lax.ppermute(queries, "inst", core_pairs)
@@ -309,7 +311,7 @@
             pltpu.VMEM((steps, width), jnp.bfloat16),
             pltpu.VMEM((3, heads, HD), jnp.float32),
             pltpu.VMEM((2, HD, width), jnp.bfloat16),
-            pltpu.SMEM((3 + 2 * slots,), jnp.int32),
+            pltpu.SMEM((4 + 2 * slots,), jnp.int32),
         ],
         in_specs=[SMEM] + [HBM] * 6,
         out_specs=[VMEM] * 3 + [SMEM],
@@ -338,7 +340,7 @@
         ),
         name="spread",
     )(plan, near(query), other)
-    asked = over_chips(spread)
+    asked = over_chips(spread, ASK_ORDER)
     sent_cols = 2 * width + HD
     partial = pl.pallas_call(
         attend_kernel,
@@ -355,10 +357,10 @@
         ),
         name="attend",
     )(plan, asked, near(query), near(fresh), near(key_blocks), near(value_blocks))
-    everyone = over_chips(partial)
+    everyone = over_chips(partial, SEND_ORDER)
     everyone = everyone.reshape(chips * steps, sent_cols)
     share = pl.pallas_call(
-        functools.partial(project_kernel, steps, 2 + 2 * slots),
+        functools.partial(project_kernel, steps, 3 + 2 * slots),
         out_shape=jax.ShapeDtypeStruct(
             (shares, devices * steps // shares, out_weight.shape[1]), jnp.bfloat16
         ),

time: 47.9 us -> 43.5 us (0.908)
  blocking collectives: 35.5 us -> 31.3 us
    all_to_all x1, blocking collectives: 14.6 us -> 12 us  [body(): lax.all_to_all(share, 'tp', 0, 0, tiled=True, axis_index_groups=[TP_ORDER])]
    all_to_all x2, blocking collectives: 20.9 us -> 19.3 us  [over_chips(): lax.all_to_all(x, 'inst', 0, 0, tiled=True, axis_index_groups=same_core)]
  transfers between devices with their start and end apart: 2 -> 2, of which waited for: 2 -> 1; matrix products, arithmetic and copies ran while one was open for 0% -> 0% of each run, Pallas kernels for 2% -> 2%
where the time goes in v4:
time: 43.5 us; the launch traced here: 43.3 us
  blocking collectives  31.3 us (72%)
  starting transfers between devices  6.03 us (14%)
  Pallas kernels  4.59 us (11%)
  waiting for transfers between devices  1.23 us (3%)
    all_to_all x2, blocking collectives, over_chips(): lax.all_to_all(x, 'inst', 0, 0, tiled=True, axis_index_groups=same_core)  19.3 us
    all_to_all x1, blocking collectives, body(): lax.all_to_all(share, 'tp', 0, 0, tiled=True, axis_index_groups=[TP_ORDER])  12 us
    ppermute x1, starting transfers between devices, body(): other = lax.ppermute(queries, 'inst', core_pairs)  3.24 us
    ppermute x1, starting transfers between devices, body(): lax.ppermute(everyone, 'inst', core_pairs)  2.79 us
    pallas_call x1, Pallas kernels, body(): pl.pallas_call(attend_kernel, out_shape=pltpu.VMEM((chips, steps, sent_co...  2.4 us
    ppermute x1, waiting for transfers between devices, body(): lax.ppermute(everyone, 'inst', core_pairs)  1.19 us
    pallas_call x1, Pallas kernels, body(): pl.pallas_call(functools.partial(plan_kernel, block_len), out_shape=[pltp...  0.98 us
  transfers between devices with their start and end apart: 2, of which 1 were waited for; matrix products, arithmetic and copies ran while one was open for 0% of the time, Pallas kernels for 2%

profile of v4, /device:TPU:1, one launch (start us, length us, event | category | flops | bytes accessed | tf_op | source)
XLA Modules:
  0.0 43.3 jit_solution(17381379035864112251)
XLA Ops:
  0.0 3.2 %collective-permute-start = (bf16[1,4,1024]{2,1,0:T(4,128)(2,1)}, bf16[1,4,1024]{2,1,0:T(4,128)(2,1)S(1)}, u32[]{:S(2)}, u32[]{:S(2)}) collective-permute-start(bf16[1,4,1024]{2,1,0:T(4,128)(2,1)} %query_hbm.1), channel_id=1, source_target_pairs={{0,8},{8,0},{16,24},{24,16},{32,40},{40,32},{48,56},{56,48},{64,72... | collective-permute-start | bytes 24584 | tf_op jit(solution)/shard_map/ppermute | solution.py:307
  3.2 1.0 %plan.1 = (bf16[4,1024]{1,0:T(4,128)(2,1)S(1)}, f32[3,32,128]{2,1,0:T(8,128)S(1)}, bf16[2,128,1024]{2,1,0:T(8,128)(2,1)S(1)}, s32[20]{0:T(128)S(4)}) custom-call(s32[1]{0:T(128)} %bitcast.me_ref, s32[8]{0:T(128)} %rows_hbm.1, s32[8]{0:T(128)} %blocks_hbm.1, s32[32]{0:T(128)} %lengths_hbm.1, bf16[1,4,1024]{2,1,0:T(4,128)(2,1)} %query_hbm.1, ...), custom_call_target="tpu_custom_call" | custom-call | flops 1000000 | bytes 3000000 | tf_op jit(solution)/shard_map/plan/pallas_call | solution.py:308
  4.2 0.0 collective-permute-done.other_ref
  4.3 0.0 copy-start
  4.3 0.0 copy-start.1
  4.3 9.1 %all_to_all.15.asked_ref = bf16[16,4,1024]{2,1,0:T(4,128)(2,1)S(1)} all-to-all(bf16[16,4,1024]{2,1,0:T(4,128)(2,1)S(1)} %spread.1), channel_id=1, replica_groups={{160,176,128,144,240,192,208,224,0,16,32,48,80,96,112,64},{168,184,136,..., dimensions={0} | all-to-all | bytes 262144 | tf_op jit(solution)/shard_map/all_to_all | solution.py:305
  13.4 0.0 copy-done
  13.4 0.0 copy-done.1
  13.4 0.0 copy-start.2
  13.4 2.4 %attend.1 = bf16[16,4,2176]{2,1,0:T(4,128)(2,1)S(1)} custom-call(s32[20]{0:T(128)S(4)} %get-tuple-element.9.plan_ref, bf16[16,4,1024]{2,1,0:T(4,128)(2,1)S(1)} %all_to_all.15.asked_ref, bf16[4,1024]{1,0:T(4,128)(2,1)S(1)} %get-tuple-element.11.query_ref, f32[3,32,128]{2,1,0:T(8,128)S(1)} %get-tuple-element.12.fresh_ref, bf16[8,2048,128]{2,1,0:T(8,128)(2,1)S(1)} %copy-done, ...), custom_call_target="tpu_custom_call" | custom-call | flops 300000000 | bytes 9000000 | tf_op jit(solution)/shard_map/attend/pallas_call | solution.py:345
  15.8 10.3 %all_to_all.16 = bf16[16,4,2176]{2,1,0:T(4,128)(2,1)S(1)} all-to-all(bf16[16,4,2176]{2,1,0:T(4,128)(2,1)S(1)} %attend.1), channel_id=1, replica_groups={{160,176,80,240,128,208,112,96,16,32,224,192,144,0,48,64},{168,184,88,2..., dimensions={0} | all-to-all | bytes 557056 | tf_op jit(solution)/shard_map/all_to_all | solution.py:305
  26.1 0.1 reshape.7.mine_ref
  26.1 2.8 %collective-permute-start.1 = (bf16[64,2176]{1,0:T(8,128)(2,1)S(1)}, bf16[64,2176]{1,0:T(8,128)(2,1)S(1)}, u32[]{:S(2)}, u32[]{:S(2)}) collective-permute-start(bf16[64,2176]{1,0:T(8,128)(2,1)S(1)} %reshape.7.mine_ref), channel_id=1, source_target_pairs={{0,8},{8,0},{16,24},{24,16},{32,40},{40,32},{48,56},{56,48},{64,72... | collective-permute-start | bytes 835592 | tf_op jit(solution)/shard_map/ppermute | solution.py:371
  28.9 1.2 %collective-permute-done.1.other_ref = bf16[64,2176]{1,0:T(8,128)(2,1)S(1)} collective-permute-done((bf16[64,2176]{1,0:T(8,128)(2,1)S(1)}, bf16[64,2176]{1,0:T(8,128)(2,1)S(1)}, u32[]{:S(2)}, u32[]{:S(2)}) %collective-permute-start.1) | collective-permute-done | bytes 278560 | tf_op jit(solution)/shard_map/ppermute | solution.py:371
  30.1 0.0 copy-done.2
  30.1 0.6 %project.1 = bf16[8,16,256]{2,1,0:T(8,128)(2,1)S(1)} custom-call(s32[20]{0:T(128)S(4)} %get-tuple-element.9.plan_ref, bf16[2,128,1024]{2,1,0:T(8,128)(2,1)S(1)} %get-tuple-element.10.picks_ref, bf16[64,2176]{1,0:T(8,128)(2,1)S(1)} %reshape.7.mine_ref, bf16[64,2176]{1,0:T(8,128)(2,1)S(1)} %collective-permute-done.1.other_ref, bf16[1024,256]{1,0:T(8,128)(2,1)S(1)} %copy-done.2), custom_call_target="tpu_custom_call" | custom-call | tf_op jit(solution)/shard_map/project/pallas_call | solution.py:362
  30.7 12.0 %all_to_all.17.shares_ref = bf16[8,16,256]{2,1,0:T(8,128)(2,1)S(1)} all-to-all(bf16[8,16,256]{2,1,0:T(8,128)(2,1)S(1)} %project.1), channel_id=1, replica_groups={{4,6,1,3,5,7,0,2},{12,14,9,11,13,15,8,10},{20,22,17,19,21,23,16,18},{28..., dimensions={0} | all-to-all | bytes 131072 | tf_op jit(solution)/shard_map/all_to_all | solution.py:372
  42.7 0.6 %add.1 = bf16[4,4,256]{2,1,0:T(4,128)(2,1)} custom-call(bf16[8,16,256]{2,1,0:T(8,128)(2,1)S(1)} %all_to_all.17.shares_ref), custom_call_target="tpu_custom_call" | custom-call | tf_op jit(solution)/shard_map/add/pallas_call | solution.py:373
  (1 shorter events, 0.0 us)
Async XLA Ops:
  0.0 4.3 %collective-permute-start = (bf16[1,4,1024]{2,1,0:T(4,128)(2,1)}, bf16[1,4,1024]{2,1,0:T(4,128)(2,1)S(1)}, u32[]{:S(2)}, u32[]{:S(2)}) collective-permute-start(bf16[1,4,1024]{2,1,0:T(4,128)(2,1)} %query_hbm.1), channel_id=1, source_target_pairs={{0,8},{8,0},{16,24},{24,16},{32,40},{40,32},{48,56},{56,48},{64,72... | collective-permute-start | bytes 24584 | tf_op jit(solution)/shard_map/ppermute | solution.py:307
  4.3 9.1 %copy-start = (bf16[8,2048,128]{2,1,0:T(8,128)(2,1)S(1)}, bf16[8,2048,128]{2,1,0:T(8,128)(2,1)}, u32[]{:S(2)}) copy-start(bf16[8,2048,128]{2,1,0:T(8,128)(2,1)} %key_ref.1) | copy-start | bytes 12582916
  4.3 9.1 %copy-start.1 = (bf16[8,2048,128]{2,1,0:T(8,128)(2,1)S(1)}, bf16[8,2048,128]{2,1,0:T(8,128)(2,1)}, u32[]{:S(2)}) copy-start(bf16[8,2048,128]{2,1,0:T(8,128)(2,1)} %value_ref.1) | copy-start | bytes 12582916
  13.4 16.7 %copy-start.2 = (bf16[1024,256]{1,0:T(8,128)(2,1)S(1)}, bf16[1024,256]{1,0:T(8,128)(2,1)}, u32[]{:S(2)}) copy-start(bf16[1024,256]{1,0:T(8,128)(2,1)} %weight_ref.1) | copy-start | bytes 1572868
  26.1 4.0 %collective-permute-start.1 = (bf16[64,2176]{1,0:T(8,128)(2,1)S(1)}, bf16[64,2176]{1,0:T(8,128)(2,1)S(1)}, u32[]{:S(2)}, u32[]{:S(2)}) collective-permute-start(bf16[64,2176]{1,0:T(8,128)(2,1)S(1)} %reshape.7.mine_ref), channel_id=1, source_target_pairs={{0,8},{8,0},{16,24},{24,16},{32,40},{40,32},{48,56},{56,48},{64,72... | collective-permute-start | bytes 835592 | tf_op jit(solution)/shard_map/ppermute | solution.py:371

commit v5 on v4

--- a/solution.py
+++ b/solution.py
@@ -16,9 +16,11 @@
 C = HD ** (-0.5) / math.log(2.0)
 PIECES = 3
 CORES = 2
+UNITS = 2
+MXU = 256
 ASK_ORDER = [10, 11, 8, 9, 15, 12, 13, 14, 0, 1, 2, 3, 5, 6, 7, 4]
-SEND_ORDER = [10, 11, 5, 15, 8, 13, 7, 6, 1, 2, 14, 12, 9, 0, 3, 4]
-TP_ORDER = [4, 6, 1, 3, 5, 7, 0, 2]
+SEND_ORDER = [10, 11, 8, 9, 15, 12, 13, 14, 0, 1, 2, 3, 5, 6, 7, 4]
+TP_ORDER = [4, 0, 5, 1, 6, 2, 7, 3]
 
 
 def longest_row(lengths_ref):
@@ -138,7 +140,15 @@
     spread_ref[...] = jnp.broadcast_to(asked[None], spread_ref.shape)
 
 
-def attend_kernel(
+def attend_kernel(*refs):
+    rows = 2 * refs[-2].shape[1]
+    pl.run_scoped(
+        lambda *sums: attend(*refs, [sums[: len(sums) // UNITS], sums[len(sums) // UNITS :]]),
+        *[pltpu.ACC(unit)((rows, MXU), jnp.float32) for unit in range(UNITS) for _ in range(4)],
+    )
+
+
+def attend(
     plan_ref,
     asked_ref,
     query_ref,
@@ -148,6 +158,7 @@
     out_ref,
     queries,
     scores,
+    sums,
 ):
     slots, block_len, _ = key_ref.shape
     steps = query_ref.shape[0]
@@ -157,28 +168,66 @@
     queries[0] = rows_of_heads(query_ref[...].astype(jnp.float32)).astype(jnp.bfloat16)
     queries[1] = rows_of_heads(asked_ref[plan_ref[2 + 2 * slots]].astype(jnp.float32)).astype(jnp.bfloat16)
 
-    column = lax.broadcasted_iota(jnp.int32, (heads, block_len), 1)
-    tops = []
-    for s in range(slots):
-        score = lax.dot_general(
-            queries[plan_ref[2 + s]],
-            key_ref[s],
-            (((1,), (1,)), ((), ())),
-            preferred_element_type=jnp.float32,
-        )
-        score = jnp.where(column < plan_ref[2 + slots + s], score, NEG)
-        scores[s] = score
-        tops.append(jnp.maximum(jnp.max(score, axis=1, keepdims=True), FLOOR))
+    tiles = block_len // MXU
+    column = lax.broadcasted_iota(jnp.int32, (heads, MXU), 1)
+    high = {}
+
+    def keep(s, tile, product):
+        for k in range(2):
+            score = product[k * heads : (k + 1) * heads]
+            valid = plan_ref[2 + slots + s + k] - tile * MXU
+            score = jnp.where(column < valid, score, NEG)
+            scores[s + k, :, tile * MXU : (tile + 1) * MXU] = score
+            most = functools.reduce(
+                jnp.maximum, [score[:, at : at + HD] for at in range(0, MXU, HD)]
+            )
+            high[s + k] = jnp.maximum(high[s + k], most) if s + k in high else most
+
+    pending = []
+    for n, (s, tile) in enumerate((s, t) for s in range(0, slots, 2) for t in range(tiles)):
+        if tile == 0:
+            first, second = queries[plan_ref[2 + s]], queries[plan_ref[3 + s]]
+            none = jnp.zeros_like(first)
+            query = jnp.concatenate(
+                [
+                    jnp.concatenate([first, none], axis=1),
+                    jnp.concatenate([none, second], axis=1),
+                ],
+                axis=0,
+            )
+        unit, turn = n % UNITS, n // UNITS
+        rows = slice(tile * MXU, (tile + 1) * MXU)
+        both = jnp.concatenate([key_ref[s, rows], key_ref[s + 1, rows]], axis=1)
+        pltpu.matmul_push_rhs(both, turn % 2, unit, transpose=True)
+        into = sums[unit][turn % len(sums[unit])]
+        pltpu.matmul_acc_lhs(into, query, load_staged_rhs=turn % 2)
+        pending.append((s, tile, into))
+        if len(pending) > UNITS * (len(sums[unit]) - 1):
+            then, at, done = pending.pop(0)
+            keep(then, at, pltpu.matmul_pop(done))
+    for then, at, done in pending:
+        keep(then, at, pltpu.matmul_pop(done))
+    tops = [
+        jnp.maximum(jnp.max(high[s], axis=1, keepdims=True), FLOOR) for s in range(slots)
+    ]
 
     parts = [(mine, fresh_ref[0][:, :1], fresh_ref[1][:, :1], fresh_ref[2])]
 
-    for s in range(slots):
-        weights = jnp.exp2((scores[s] - tops[s]) * C)
-        total = jnp.sum(weights, axis=1, keepdims=True)
-        acc = jnp.dot(
-            weights.astype(jnp.bfloat16), value_ref[s], preferred_element_type=jnp.float32
-        )
-        parts.append((plan_ref[2 + s] == 1, tops[s], total, acc))
+    for s in range(0, slots, 2):
+        weights = [jnp.exp2((scores[s + k] - tops[s + k]) * C) for k in range(2)]
+        rounded = jnp.concatenate(weights, axis=0).astype(jnp.bfloat16)
+        turn = s // 2 % 2
+        for tile in range(tiles):
+            rows = slice(tile * MXU, (tile + 1) * MXU)
+            both = jnp.concatenate([value_ref[s, rows], value_ref[s + 1, rows]], axis=1)
+            unit, stage = tile % UNITS, tile // UNITS % 2
+            pltpu.matmul_push_rhs(both, stage, unit)
+            pltpu.matmul_acc_lhs(sums[unit][turn], rounded[:, rows], load_staged_rhs=stage)
+        product = sum(pltpu.matmul_pop(sums[unit][turn]) for unit in range(UNITS))
+        for k in range(2):
+            acc = product[k * heads : (k + 1) * heads, k * HD : (k + 1) * HD]
+            total = jnp.sum(weights[k], axis=1, keepdims=True)
+            parts.append((plan_ref[2 + s + k] == 1, tops[s + k], total, acc))
 
     merged = []
     for wanted in (False, True):

time: 43.5 us -> 43.1 us (level)
  transfers between devices with their start and end apart: 2 -> 2, of which waited for: 1 -> 2; matrix products, arithmetic and copies ran while one was open for 0% -> 0% of each run, Pallas kernels for 2% -> 2%
where the time goes in v5:
time: 43.1 us; the launch traced here: 42.9 us
  blocking collectives  30.9 us (72%)
  starting transfers between devices  6.19 us (14%)
  Pallas kernels  4.45 us (10%)
  waiting for transfers between devices  1.24 us (3%)
    all_to_all x2, blocking collectives, over_chips(): lax.all_to_all(x, 'inst', 0, 0, tiled=True, axis_index_groups=same_core)  19 us
    all_to_all x1, blocking collectives, body(): lax.all_to_all(share, 'tp', 0, 0, tiled=True, axis_index_groups=[TP_ORDER])  11.9 us
    ppermute x1, starting transfers between devices, body(): other = lax.ppermute(queries, 'inst', core_pairs)  3.24 us
    ppermute x1, starting transfers between devices, body(): lax.ppermute(everyone, 'inst', core_pairs)  2.95 us
    pallas_call x1, Pallas kernels, body(): pl.pallas_call(attend_kernel, out_shape=pltpu.VMEM((chips, steps, sent_co...  2.26 us
    ppermute x1, waiting for transfers between devices, body(): lax.ppermute(everyone, 'inst', core_pairs)  1.19 us
    pallas_call x1, Pallas kernels, body(): pl.pallas_call(functools.partial(plan_kernel, block_len), out_shape=[pltp...  0.98 us
  transfers between devices with their start and end apart: 2, of which 2 were waited for; matrix products, arithmetic and copies ran while one was open for 0% of the time, Pallas kernels for 2%

profile of v5, /device:TPU:1, one launch (start us, length us, event | category | flops | bytes accessed | tf_op | source)
XLA Modules:
  0.0 42.9 jit_solution(16598103583567217029)
XLA Ops:
  0.0 3.2 %collective-permute-start = (bf16[1,4,1024]{2,1,0:T(4,128)(2,1)}, bf16[1,4,1024]{2,1,0:T(4,128)(2,1)S(1)}, u32[]{:S(2)}, u32[]{:S(2)}) collective-permute-start(bf16[1,4,1024]{2,1,0:T(4,128)(2,1)} %query_hbm.1), channel_id=1, source_target_pairs={{0,8},{8,0},{16,24},{24,16},{32,40},{40,32},{48,56},{56,48},{64,72... | collective-permute-start | bytes 24584 | tf_op jit(solution)/shard_map/ppermute | solution.py:356
  3.2 1.0 %plan.1 = (bf16[4,1024]{1,0:T(4,128)(2,1)S(1)}, f32[3,32,128]{2,1,0:T(8,128)S(1)}, bf16[2,128,1024]{2,1,0:T(8,128)(2,1)S(1)}, s32[20]{0:T(128)S(4)}) custom-call(s32[1]{0:T(128)} %bitcast.me_ref, s32[8]{0:T(128)} %rows_hbm.1, s32[8]{0:T(128)} %blocks_hbm.1, s32[32]{0:T(128)} %lengths_hbm.1, bf16[1,4,1024]{2,1,0:T(4,128)(2,1)} %query_hbm.1, ...), custom_call_target="tpu_custom_call" | custom-call | flops 1000000 | bytes 3000000 | tf_op jit(solution)/shard_map/plan/pallas_call | solution.py:357
  4.2 0.1 collective-permute-done.other_ref
  4.3 0.0 copy-start
  4.3 0.0 copy-start.1
  4.3 9.1 %all_to_all.15.refs_1_ = bf16[16,4,1024]{2,1,0:T(4,128)(2,1)S(1)} all-to-all(bf16[16,4,1024]{2,1,0:T(4,128)(2,1)S(1)} %spread.1), channel_id=1, replica_groups={{160,176,128,144,240,192,208,224,0,16,32,48,80,96,112,64},{168,184,136,..., dimensions={0} | all-to-all | bytes 262144 | tf_op jit(solution)/shard_map/all_to_all | solution.py:354
  13.4 0.0 copy-done
  13.4 0.0 copy-done.1
  13.4 0.0 copy-start.2
  13.4 2.3 %attend.1 = bf16[16,4,2176]{2,1,0:T(4,128)(2,1)S(1)} custom-call(s32[20]{0:T(128)S(4)} %get-tuple-element.9.plan_ref.refs_0_, bf16[16,4,1024]{2,1,0:T(4,128)(2,1)S(1)} %all_to_all.15.refs_1_, bf16[4,1024]{1,0:T(4,128)(2,1)S(1)} %get-tuple-element.11.query_ref.refs_2_, f32[3,32,128]{2,1,0:T(8,128)S(1)} %get-tuple-element.12.refs_3_, ...), custom_call_target="tpu_custom_call" | custom-call | flops 300000000 | bytes 9000000 | tf_op jit(solution)/shard_map/attend/pallas_call | solution.py:394
  15.6 9.9 %all_to_all.16 = bf16[16,4,2176]{2,1,0:T(4,128)(2,1)S(1)} all-to-all(bf16[16,4,2176]{2,1,0:T(4,128)(2,1)S(1)} %attend.1), channel_id=1, replica_groups={{160,176,128,144,240,192,208,224,0,16,32,48,80,96,112,64},{168,184,136,..., dimensions={0} | all-to-all | bytes 557056 | tf_op jit(solution)/shard_map/all_to_all | solution.py:354
  25.6 0.1 reshape.7.mine_ref
  25.7 3.0 %collective-permute-start.1 = (bf16[64,2176]{1,0:T(8,128)(2,1)S(1)}, bf16[64,2176]{1,0:T(8,128)(2,1)S(1)}, u32[]{:S(2)}, u32[]{:S(2)}) collective-permute-start(bf16[64,2176]{1,0:T(8,128)(2,1)S(1)} %reshape.7.mine_ref), channel_id=1, source_target_pairs={{0,8},{8,0},{16,24},{24,16},{32,40},{40,32},{48,56},{56,48},{64,72... | collective-permute-start | bytes 835592 | tf_op jit(solution)/shard_map/ppermute | solution.py:420
  28.6 1.2 %collective-permute-done.1.other_ref = bf16[64,2176]{1,0:T(8,128)(2,1)S(1)} collective-permute-done((bf16[64,2176]{1,0:T(8,128)(2,1)S(1)}, bf16[64,2176]{1,0:T(8,128)(2,1)S(1)}, u32[]{:S(2)}, u32[]{:S(2)}) %collective-permute-start.1) | collective-permute-done | bytes 278560 | tf_op jit(solution)/shard_map/ppermute | solution.py:420
  29.8 0.0 copy-done.2
  29.8 0.6 %project.1 = bf16[8,16,256]{2,1,0:T(8,128)(2,1)S(1)} custom-call(s32[20]{0:T(128)S(4)} %get-tuple-element.9.plan_ref.refs_0_, bf16[2,128,1024]{2,1,0:T(8,128)(2,1)S(1)} %get-tuple-element.10.picks_ref, bf16[64,2176]{1,0:T(8,128)(2,1)S(1)} %reshape.7.mine_ref, bf16[64,2176]{1,0:T(8,128)(2,1)S(1)} %collective-permute-done.1.other_ref, ...), custom_call_target="tpu_custom_call" | custom-call | tf_op jit(solution)/shard_map/project/pallas_call | solution.py:411
  30.4 11.9 %all_to_all.17.shares_ref = bf16[8,16,256]{2,1,0:T(8,128)(2,1)S(1)} all-to-all(bf16[8,16,256]{2,1,0:T(8,128)(2,1)S(1)} %project.1), channel_id=1, replica_groups={{4,0,5,1,6,2,7,3},{12,8,13,9,14,10,15,11},{20,16,21,17,22,18,23,19},{28..., dimensions={0} | all-to-all | bytes 131072 | tf_op jit(solution)/shard_map/all_to_all | solution.py:421
  42.3 0.6 %add.1 = bf16[4,4,256]{2,1,0:T(4,128)(2,1)} custom-call(bf16[8,16,256]{2,1,0:T(8,128)(2,1)S(1)} %all_to_all.17.shares_ref), custom_call_target="tpu_custom_call" | custom-call | tf_op jit(solution)/shard_map/add/pallas_call | solution.py:422
  (1 shorter events, 0.0 us)
Async XLA Ops:
  0.0 4.3 %collective-permute-start = (bf16[1,4,1024]{2,1,0:T(4,128)(2,1)}, bf16[1,4,1024]{2,1,0:T(4,128)(2,1)S(1)}, u32[]{:S(2)}, u32[]{:S(2)}) collective-permute-start(bf16[1,4,1024]{2,1,0:T(4,128)(2,1)} %query_hbm.1), channel_id=1, source_target_pairs={{0,8},{8,0},{16,24},{24,16},{32,40},{40,32},{48,56},{56,48},{64,72... | collective-permute-start | bytes 24584 | tf_op jit(solution)/shard_map/ppermute | solution.py:356
  4.3 9.1 %copy-start = (bf16[8,2048,128]{2,1,0:T(8,128)(2,1)S(1)}, bf16[8,2048,128]{2,1,0:T(8,128)(2,1)}, u32[]{:S(2)}) copy-start(bf16[8,2048,128]{2,1,0:T(8,128)(2,1)} %refs_4_.1) | copy-start | bytes 12582916
  4.3 9.1 %copy-start.1 = (bf16[8,2048,128]{2,1,0:T(8,128)(2,1)S(1)}, bf16[8,2048,128]{2,1,0:T(8,128)(2,1)}, u32[]{:S(2)}) copy-start(bf16[8,2048,128]{2,1,0:T(8,128)(2,1)} %refs_5_.1) | copy-start | bytes 12582916
  13.4 16.4 %copy-start.2 = (bf16[1024,256]{1,0:T(8,128)(2,1)S(1)}, bf16[1024,256]{1,0:T(8,128)(2,1)}, u32[]{:S(2)}) copy-start(bf16[1024,256]{1,0:T(8,128)(2,1)} %weight_ref.1) | copy-start | bytes 1572868
  25.7 4.1 %collective-permute-start.1 = (bf16[64,2176]{1,0:T(8,128)(2,1)S(1)}, bf16[64,2176]{1,0:T(8,128)(2,1)S(1)}, u32[]{:S(2)}, u32[]{:S(2)}) collective-permute-start(bf16[64,2176]{1,0:T(8,128)(2,1)S(1)} %reshape.7.mine_ref), channel_id=1, source_target_pairs={{0,8},{8,0},{16,24},{24,16},{32,40},{40,32},{48,56},{56,48},{64,72... | collective-permute-start | bytes 835592 | tf_op jit(solution)/shard_map/ppermute | solution.py:420
